TPU v7x, 256 devices: a whole 4x4x8 slice. The times are simulated.
256 devices in a mesh: row: 32 (over y, z_hi, x), col: 8 (over z_lo, core).
Axes of the slice: x: 4, y: 4, z: 8 (z_hi: 2, z_lo: 4; z = z_hi * 4 + z_lo), core: 2. Of those that a mesh axis runs over, the one named last changes fastest.
Arguments:
- pair: bfloat16 [512, 512, 128], P('row', 'col'), may hold values from -6 to 6
- token_mask: int32 [512], replicated, may hold values 0 or 1
- ln_in_gain: float32 [128], replicated, may hold values from 0.25 to 1.75
- ln_in_bias: float32 [128], replicated, may hold values from -3 to 3
- w_left: bfloat16 [128, 128], replicated, may hold values from -0.5 to 0.5
- w_left_gate: bfloat16 [128, 128], replicated, may hold values from -0.5 to 0.5
- w_right: bfloat16 [128, 128], replicated, may hold values from -0.5 to 0.5
- w_right_gate: bfloat16 [128, 128], replicated, may hold values from -0.5 to 0.5
- w_gate: bfloat16 [128, 128], replicated, may hold values from -0.5 to 0.5
- ln_out_gain: float32 [128], replicated, may hold values from 0.25 to 1.75
- ln_out_bias: float32 [128], replicated, may hold values from -3 to 3
- w_out: bfloat16 [128, 128], replicated, may hold values from -0.5 to 0.5
Outputs:
- update: bfloat16 [512, 512, 128], P('row', 'col')
All inputs are finite; a program needn't handle non-finite values.
Results may differ from a plain program's by a relative error of at most 0.0054.
Values may be sent and summed in bfloat16 or wider, within the bound.
No kernel may reach another device: no remote copies, remote signals or barrier semaphores. Data moves between devices by JAX's collectives and lax.ppermute only.
A program may use at most 64 MiB of HBM per device.

v0:
```python
import jax
import jax.numpy as jnp
from jax import lax
from jax.sharding import PartitionSpec as P


def broadcast(block, axis, owner):
    block = jnp.where(lax.axis_index(axis) == owner, block, jnp.zeros_like(block))
    return lax.psum(block, axis)


def normalize(values, gain, bias):
    mean = jnp.mean(values, axis=-1, keepdims=True)
    centred = values - mean
    variance = jnp.mean(centred * centred, axis=-1, keepdims=True)
    return centred * lax.rsqrt(variance + 1e-05) * gain + bias


def shards(
    pair,
    token_mask,
    ln_in_gain,
    ln_in_bias,
    w_left,
    w_left_gate,
    w_right,
    w_right_gate,
    w_gate,
    ln_out_gain,
    ln_out_bias,
    w_out,
):
    rows_i, cols_k, channels = pair.shape
    hidden = w_left.shape[1]
    normed = normalize(pair.astype(jnp.float32), ln_in_gain, ln_in_bias).astype(jnp.bfloat16)
    flat = normed.reshape(rows_i * cols_k, channels)
    row_start = lax.axis_index("row") * rows_i
    col_start = lax.axis_index("col") * cols_k
    mask_rows = lax.dynamic_slice_in_dim(token_mask, row_start, rows_i).astype(jnp.float32)
    mask_cols = lax.dynamic_slice_in_dim(token_mask, col_start, cols_k).astype(jnp.float32)
    pair_mask = (mask_rows[:, None] * mask_cols[None, :]).reshape(rows_i * cols_k, 1)
    weights = jnp.concatenate([w_left, w_left_gate, w_right, w_right_gate], axis=1)
    projected = jnp.dot(flat, weights, preferred_element_type=jnp.float32)
    left = pair_mask * jax.nn.sigmoid(projected[:, hidden : 2 * hidden]) * projected[:, :hidden]
    right = (
        pair_mask
        * jax.nn.sigmoid(projected[:, 3 * hidden :])
        * projected[:, 2 * hidden : 3 * hidden]
    )
    left = left.astype(jnp.bfloat16).reshape(rows_i, cols_k, hidden)
    right = right.astype(jnp.bfloat16).reshape(rows_i, cols_k, hidden)
    left_full, right_full = (
        lax.all_gather(left, "col", axis=1, tiled=True),
        lax.all_gather(right, "col", axis=1, tiled=True),
    )
    ratio = lax.axis_size("row") // lax.axis_size("col")
    blocks = []
    for quarter in range(ratio):
        root = lax.axis_index("col") * ratio + quarter
        rows_block = broadcast(right_full, "row", root)
        blocks.append(
            jnp.einsum("ikc,jkc->ijc", left_full, rows_block, preferred_element_type=jnp.float32)
        )
    triangle = jnp.concatenate(blocks, axis=1)
    triangle_normed = normalize(
        triangle.reshape(rows_i * cols_k, hidden), ln_out_gain, ln_out_bias
    ).astype(jnp.bfloat16)
    gate = jax.nn.sigmoid(jnp.dot(flat, w_gate, preferred_element_type=jnp.float32))
    update = gate * jnp.dot(triangle_normed, w_out, preferred_element_type=jnp.float32)
    return update.astype(jnp.bfloat16).reshape(rows_i, cols_k, channels)


def solution(mesh):
    placed = (P("row", "col", None), P(), P(), P(), P(), P(), P(), P(), P(), P(), P(), P())
    return jax.shard_map(
        shards, mesh=mesh, in_specs=placed, out_specs=P("row", "col", None), check_vma=False
    )
```

profile of v0, /device:TPU:1, one launch (start us, length us, event | category | flops | bytes accessed | tf_op | source)
XLA Modules:
  0.0 604.4 jit_solution(8506651437619431020)
XLA Ops:
  6.5 0.8 dynamic-slice_convert_fusion.1
  7.3 0.8 dynamic-slice_convert_fusion
  8.2 1.2 convert_reduce_fusion
  9.4 1.3 fusion.6
  10.7 1.3 fusion.9
  12.1 1.2 fusion.24
  13.6 0.9 copy.18
  14.6 0.9 copy.20
  15.5 40.5 %all-gather.3.cloned.1.call-done = bf16[16,512,128]{2,0,1:T(8,128)(2,1)} async-done(((bf16[16,64,128]{2,0,1:T(8,128)(2,1)}), bf16[16,512,128]{2,0,1:T(8,128)(2,1)}) %all-gather.3.cloned.1.call-update) | async-done | bytes 2097168 | tf_op jit(solution)/shard_map/all_gather | solution.py:54
  56.0 3.9 copy.19
  60.0 3.4 broadcast_select_fusion.3
  63.7 32.7 %all-gather.5.cloned.1.call-done = bf16[16,512,128]{2,0,1:T(8,128)(2,1)} async-done(((bf16[16,64,128]{2,0,1:T(8,128)(2,1)}), bf16[16,512,128]{2,0,1:T(8,128)(2,1)}) %all-gather.5.cloned.1.call-update) | async-done | bytes 2097168 | tf_op jit(solution)/shard_map/all_gather | solution.py:53
  96.4 3.9 copy.21
  100.4 487.8 %all-reduce.3.cloned.1.call-done = (bf16[16,512,128]{1,0,2:T(8,128)(2,1)}, bf16[16,512,128]{1,0,2:T(8,128)(2,1)}, bf16[16,512,128]{1,0,2:T(8,128)(2,1)}, bf16[16,512,128]{1,0,2:T(8,128)(2,1)}) async-done(((bf16[16,512,128]{1,0,2:T(8,128)(2,1)}, bf16[16,512,128]{1,0,2:T(8,128)(2,1)}, bf16[16,512,128]{1,0,2:T(8,128)(2,1)}, bf16[16,512,128]{1,0,2:T(8,128)(2,1)}), (bf16[16,512,128]{1,0,2:T(8,128)(2,1)}, ...) | async-done | bytes 8388624 | tf_op jit(solution)/shard_map/psum | solution.py:9
  588.2 2.6 convolution_bitcast_fusion.3
  590.8 0.9 convolution_bitcast_fusion.2
  591.7 0.7 copy-done.2
  592.4 0.9 convolution_bitcast_fusion.1
  593.3 0.7 copy-done.1
  594.0 0.9 convolution_bitcast_fusion
  594.9 0.9 fusion.33
  595.9 0.4 copy.28
  596.6 0.3 fusion.23
  597.0 0.9 fusion.3
  (29 shorter events, 1.3 us)
Async XLA Ops:
  6.5 56.9 %copy-start = (bf16[128,128]{1,0:T(8,128)(2,1)S(1)}, bf16[128,128]{1,0:T(8,128)(2,1)}, u32[]{:S(2)}) copy-start(bf16[128,128]{1,0:T(8,128)(2,1)} %param.20) | copy-start | bytes 98308
  6.5 49.5 %all-gather.3.cloned.1.call-start = ((), (), s32[]{:S(2)}) async-start(), calls=%async_computation | async-start | bytes 2359296 | tf_op jit(solution)/shard_map/all_gather | solution.py:54
  14.5 81.9 %all-gather.5.cloned.1.call-start = ((), (), s32[]{:S(2)}) async-start(), calls=%async_computation.1 | async-start | bytes 2359296 | tf_op jit(solution)/shard_map/all_gather | solution.py:53
  15.5 572.7 %all-reduce.3.cloned.1.call-start = ((), (), s32[]{:S(2)}) async-start(), calls=%async_computation.2 | async-start | bytes 16777216 | tf_op jit(solution)/shard_map/psum | solution.py:9
  588.2 2.6 copy-start.3
  590.8 1.6 copy-start.2
  592.4 1.6 copy-start.1
  595.8 0.8 copy-start.5
  595.8 0.8 copy-start.6
  595.8 1.1 copy-start.4
Sparse Core Ops, SparseCore 0:
  14.6 41.3 all-gather.2
  57.8 38.5 all-gather.4
  99.3 488.8 all-reduce.2
where the time goes:
time: 610 us; the launch traced here: 604 us
  waiting for transfers between devices  561 us (92%)
  between operations  13.3 us (2%)
  local copies, waits for them, and re-layouts  11.7 us (2%)
  other arithmetic  10.6 us (2%)
  matrix products  7.73 us (1%)
    psum x1, waiting for transfers between devices, broadcast(): return lax.psum(block, axis)  488 us
    all_gather x1, waiting for transfers between devices, shards(): lax.all_gather(right, 'col', axis=1, tiled=True)  40.5 us
    all_gather x1, waiting for transfers between devices, shards(): lax.all_gather(left, 'col', axis=1, tiled=True)  32.7 us
  transfers between devices with their start and end apart: 3, of which 3 were waited for; matrix products, arithmetic and copies ran while one was open for 2% of the time, Pallas kernels for 0%

commit v1 on v0

v1 whole, which is shorter than its diff:
```python
import jax
import jax.numpy as jnp
from jax import lax
from jax.experimental import pallas as pl
from jax.experimental.pallas import tpu as pltpu
from jax.sharding import Mesh, PartitionSpec as P

F32 = jnp.float32
BF16 = jnp.bfloat16
NT = (((1,), (1,)), ((), ()))
TN = (((0,), (0,)), ((), ()))
PARAMS = pltpu.CompilerParams(vmem_limit_bytes=24 * 1024 * 1024)
VMEM = pl.BlockSpec(memory_space=pltpu.VMEM)
SMEM = pl.BlockSpec(memory_space=pltpu.SMEM)


def low_lanes(shape):
    return lax.broadcasted_iota(jnp.int32, shape, len(shape) - 1) < 64


def project(
    mask_scalars, mask_rows, x_ref, gain, bias, w_l, w_lg, w_r, w_rg, out_ref, normed_ref, rows
):
    row, core = lax.axis_index("row"), lax.axis_index("core")
    x = x_ref[...].astype(F32)
    centred = x - jnp.mean(x, axis=-1, keepdims=True)
    variance = jnp.mean(centred * centred, axis=-1, keepdims=True)
    normed = (centred * lax.rsqrt(variance + 1e-05) * gain[...] + bias[...]).astype(BF16)
    normed_ref[...] = normed
    weights = jnp.concatenate([w[...].T for w in (w_l, w_lg, w_r, w_rg)], axis=0)
    mask_k = mask_rows[pl.ds(lax.axis_index("zl"), 1), :].astype(F32)
    swapped = pltpu.roll(mask_k, 64, 1)
    low = low_lanes((1, 128))
    mask_k = jnp.where(low == (core == 0), mask_k, swapped)
    for s in range(8):
        tokens = jnp.concatenate([normed[s], normed[s + 8]], axis=0)
        p = lax.dot_general(weights, tokens, NT, preferred_element_type=F32)
        mask_a = mask_scalars[row * 16 + s].astype(F32)
        mask_b = mask_scalars[row * 16 + s + 8].astype(F32)
        mask = mask_k * jnp.where(low, mask_a, mask_b)
        left = mask * jax.nn.sigmoid(p[128:256]) * p[:128]
        right = mask * jax.nn.sigmoid(p[384:]) * p[256:384]
        rows[pl.ds(s, 128, stride=16), :] = left
        rows[pl.ds(8 + s, 128, stride=16), :] = right
    out_ref[...] = rows[...].reshape(128, 16, 128).astype(BF16)


def contract(s_ref, keep_ref, send_ref):
    core = lax.axis_index("core")
    edges = s_ref[...].astype(F32).reshape(32, 4, 16, 128)
    low = low_lanes((256, 128))
    left_a, left_b, right, swapped = [], [], [], []
    for z in range(4):
        left_z = edges[:, z, :8].reshape(256, 128)
        right_z = edges[:, z, 8:].reshape(256, 128)
        left_a.append(jnp.where(low, left_z, 0.0).astype(BF16))
        left_b.append(jnp.where(low, 0.0, left_z).astype(BF16))
        right.append(right_z.astype(BF16))
        swapped.append(pltpu.roll(right_z, 64, 1).astype(BF16))
    left = jnp.concatenate(
        [jnp.concatenate(left_a, axis=1), jnp.concatenate(left_b, axis=1)], axis=0
    )
    right = jnp.concatenate(right, axis=1).reshape(4, 2, 32, 512)
    swapped = jnp.concatenate(swapped, axis=1).reshape(4, 2, 32, 512)
    both = jnp.concatenate([right, swapped], axis=2)
    first, second = both[:, 0].reshape(256, 512), both[:, 1].reshape(256, 512)
    mine = jnp.where(core == 0, first, second)
    other = jnp.where(core == 0, second, first)
    send_ref[...] = lax.dot_general(left, other, NT, preferred_element_type=F32)
    keep_ref[...] = lax.dot_general(left, mine, NT, preferred_element_type=F32)


def add_halves(keep_ref, got_ref, out_ref):
    low = low_lanes((256, 128))
    for v in range(2):
        cols = slice(128 * v, 128 * v + 128)
        a = keep_ref[:256, cols] + got_ref[:256, cols]
        b = keep_ref[256:, cols] + got_ref[256:, cols]
        even = jnp.where(low, a, pltpu.roll(b, 64, 1))
        odd = jnp.where(low, pltpu.roll(a, 64, 1), b)
        out_ref[:, 2 * v] = even.reshape(32, 8, 128).astype(BF16)
        out_ref[:, 2 * v + 1] = odd.reshape(32, 8, 128).astype(BF16)


def finish(t_ref, normed_ref, w_gate, gain, bias, w_out, out_ref, rows):
    t = t_ref[...].astype(F32)
    centred = t - jnp.mean(t, axis=0, keepdims=True)
    variance = jnp.mean(centred * centred, axis=0, keepdims=True)
    rows[...] = (centred * lax.rsqrt(variance + 1e-05)).reshape(1024, 128)
    gain_col = jnp.broadcast_to(gain[...], (128, 128)).T
    bias_col = jnp.broadcast_to(bias[...], (128, 128)).T
    w = w_out[...]
    for s in range(8):
        n = (rows[pl.ds(s, 128, stride=8), :] * gain_col + bias_col).astype(BF16)
        y = lax.dot_general(n, w, TN, preferred_element_type=F32).reshape(2, 2, 4, 8, 128)
        for b in range(2):
            i = s + 8 * b
            gate = jax.nn.sigmoid(
                jnp.dot(normed_ref[i], w_gate[...], preferred_element_type=F32)
            )
            token = jnp.stack([y[b, b], y[b, 1 - b]], axis=1).reshape(64, 128)
            out_ref[i] = (gate * token).astype(BF16)


def call(kernel, outs, specs, scratch=()):
    return pl.pallas_call(
        kernel,
        out_shape=outs,
        in_specs=specs,
        out_specs=jax.tree.map(lambda _: VMEM, outs),
        scratch_shapes=scratch,
        compiler_params=PARAMS,
    )


def shape(*dims, dtype=BF16):
    return jax.ShapeDtypeStruct(dims, dtype)


def shards(
    pair,
    token_mask,
    ln_in_gain,
    ln_in_bias,
    w_left,
    w_left_gate,
    w_right,
    w_right_gate,
    w_gate,
    ln_out_gain,
    ln_out_bias,
    w_out,
):
    edges, normed = call(
        project,
        (shape(128, 16, 128), shape(16, 64, 128)),
        [SMEM] + [VMEM] * 8,
        [pltpu.VMEM((2048, 128), F32)],
    )(
        token_mask,
        token_mask.reshape(4, 128),
        pair,
        ln_in_gain.reshape(1, 128),
        ln_in_bias.reshape(1, 128),
        w_left,
        w_left_gate,
        w_right,
        w_right_gate,
    )
    edges = lax.all_to_all(edges, ("row", "zl"), 0, 0, tiled=True)
    keep, send = call(
        contract, (shape(512, 256, dtype=F32), shape(512, 256, dtype=F32)), [VMEM]
    )(edges)
    got = lax.ppermute(send, "core", [(0, 1), (1, 0)])
    triangle = call(add_halves, shape(32, 4, 8, 128), [VMEM] * 2)(keep, got)
    triangle = lax.all_to_all(
        triangle.reshape(128, 8, 128), ("row", "zl"), 0, 0, tiled=True
    )
    return call(
        finish, shape(16, 64, 128), [VMEM] * 6, [pltpu.VMEM((1024, 128), F32)]
    )(
        triangle,
        normed,
        w_gate,
        ln_out_gain.reshape(1, 128),
        ln_out_bias.reshape(1, 128),
        w_out,
    )


def solution(mesh):
    fine = Mesh(mesh.devices.reshape(32, 4, 2), ("row", "zl", "core"))
    tile = P("row", ("zl", "core"), None)
    return jax.shard_map(
        shards, mesh=fine, in_specs=(tile,) + (P(),) * 11, out_specs=tile, check_vma=False
    )
```

time: 610 us -> 68.8 us (0.11)
  waiting for transfers between devices: 561 us -> 1.54 us
  blocking collectives: 0 us -> 54.6 us
  between operations: 13.3 us -> 0.05 us
  other arithmetic: 10.6 us -> 0 us
  matrix products: 7.73 us -> 0 us
  local copies, waits for them, and re-layouts: 11.7 us -> 5.34 us
    psum x1 -> x0, waiting for transfers between devices: 488 us -> none  [broadcast(): return lax.psum(block, axis)]
    all_gather x2 -> x0, waiting for transfers between devices: 73.2 us -> none  [the longest x1 40.5 us: shards(): lax.all_gather(right, 'col', axis=1, tiled=True)]
    all_to_all x0 -> x2, blocking collectives: none -> 54.6 us  [the longest x1 34.9 us: shards(): edges = lax.all_to_all(edges, ('row', 'zl'), 0, 0, tiled=True)]
    all_gather x2 -> x0, local copies, waits for them, and re-layouts: 7.83 us -> none  [the longest x1 3.92 us: shards(): lax.all_gather(right, 'col', axis=1, tiled=True)]
    dot_general x7 -> x0, matrix products: 7.73 us -> none  [the longest x4 5.3 us: shards(): jnp.einsum('ikc,jkc->ijc', left_full, rows_block, preferred_element_type=...]
  transfers between devices with their start and end apart: 3 -> 1, of which waited for: 3 -> 1; matrix products, arithmetic and copies ran while one was open for 2% -> 0% of each run, Pallas kernels for 0% -> 0%
where the time goes in v1:
time: 68.8 us; the launch traced here: 68.2 us
  blocking collectives  54.6 us (79%)
  local copies, waits for them, and re-layouts  5.34 us (8%)
  Pallas kernels  3.87 us (6%)
  starting transfers between devices  2.89 us (4%)
  waiting for transfers between devices  1.54 us (2%)
    all_to_all x1, blocking collectives, shards(): edges = lax.all_to_all(edges, ('row', 'zl'), 0, 0, tiled=True)  34.9 us
    all_to_all x1, blocking collectives, shards(): lax.all_to_all(triangle.reshape(128, 8, 128), ('row', 'zl'), 0, 0, tiled=...  19.7 us
    unnamed x24, local copies, waits for them, and re-layouts  5.34 us
    ppermute x1, starting transfers between devices, shards(): got = lax.ppermute(send, 'core', [(0, 1), (1, 0)])  2.89 us
    pallas_call x1, Pallas kernels, shards(): call(project, (shape(128, 16, 128), shape(16, 64, 128)), [SMEM] + [VMEM]...  1.74 us
    ppermute x1, waiting for transfers between devices, shards(): got = lax.ppermute(send, 'core', [(0, 1), (1, 0)])  1.54 us
    pallas_call x1, Pallas kernels, shards(): call(finish, shape(16, 64, 128), [VMEM] * 6, [pltpu.VMEM((1024, 128), F32)])  1.45 us
  transfers between devices with their start and end apart: 1, of which 1 were waited for; matrix products, arithmetic and copies ran while one was open for 0% of the time, Pallas kernels for 0%

profile of v1, /device:TPU:1, one launch (start us, length us, event | category | flops | bytes accessed | tf_op | source)
XLA Modules:
  0.0 68.2 jit_solution(17164594067159679668)
XLA Ops:
  0.0 0.0 copy-start.7
  0.0 0.0 copy-start.8
  0.0 0.7 copy-done.7
  0.7 0.0 copy-done.8
  0.7 0.0 copy-done.9
  0.7 0.9 %copy-done = bf16[16,64,128]{2,1,0:T(8,128)(2,1)S(1)} copy-done((bf16[16,64,128]{2,1,0:T(8,128)(2,1)S(1)}, bf16[16,64,128]{2,1,0:T(8,128)(2,1)}, u32[]{:S(2)}) %copy-start) | copy-done | bytes 262168
  1.6 0.8 %copy-done.1 = bf16[128,128]{1,0:T(8,128)(2,1)S(1)} copy-done((bf16[128,128]{1,0:T(8,128)(2,1)S(1)}, bf16[128,128]{1,0:T(8,128)(2,1)}, u32[]{:S(2)}) %copy-start.1) | copy-done | bytes 32792
  2.4 0.8 %copy-done.2 = bf16[128,128]{1,0:T(8,128)(2,1)S(1)} copy-done((bf16[128,128]{1,0:T(8,128)(2,1)S(1)}, bf16[128,128]{1,0:T(8,128)(2,1)}, u32[]{:S(2)}) %copy-start.2) | copy-done | bytes 32792
  3.2 0.8 %copy-done.3 = bf16[128,128]{1,0:T(8,128)(2,1)S(1)} copy-done((bf16[128,128]{1,0:T(8,128)(2,1)S(1)}, bf16[128,128]{1,0:T(8,128)(2,1)}, u32[]{:S(2)}) %copy-start.3) | copy-done | bytes 32792
  3.9 0.8 %copy-done.4 = bf16[128,128]{1,0:T(8,128)(2,1)S(1)} copy-done((bf16[128,128]{1,0:T(8,128)(2,1)S(1)}, bf16[128,128]{1,0:T(8,128)(2,1)}, u32[]{:S(2)}) %copy-start.4) | copy-done | bytes 32792
  4.7 1.7 %shard_map.118 = (bf16[128,16,128]{2,1,0:T(8,128)(2,1)S(1)}, bf16[16,64,128]{2,1,0:T(8,128)(2,1)S(1)}) custom-call(s32[512]{0:T(512)S(1)} %copy-done.7, s32[4,128]{1,0:T(4,128)S(1)} %bitcast.7, bf16[16,64,128]{2,1,0:T(8,128)(2,1)S(1)} %copy-done, f32[1,128]{1,0:T(1,128)S(1)} %bitcast.8, f32[1,128]{1,0:T(1,128)S(1)} %bitcast.9, ...), custom_call_target="tpu_custom_call" | custom-call | tf_op jit(solution)/shard_map/pallas_call | solution.py:134
  6.4 34.9 %all_to_all.10.s_ref = bf16[128,16,128]{2,1,0:T(8,128)(2,1)S(1)} all-to-all(bf16[128,16,128]{2,1,0:T(8,128)(2,1)S(1)} %get-tuple-element.9), channel_id=1, replica_groups=mesh['row'=32,'zl'=4,'core'=2] {'row','zl'}, dimensions={0} | all-to-all | bytes 1048576 | tf_op jit(solution)/shard_map/all_to_all | solution.py:150
  41.3 0.5 shard_map.119
  41.9 2.9 %collective-permute-start = (f32[512,256]{1,0:T(8,128)S(1)}, f32[512,256]{1,0:T(8,128)S(1)}, u32[]{:S(2)}, u32[]{:S(2)}) collective-permute-start(f32[512,256]{1,0:T(8,128)S(1)} %get-tuple-element.11), channel_id=1, source_target_pairs={{0,1},{1,0},{2,3},{3,2},{4,5},{5,4},{6,7},{7,6},{8,9},{9,8},{10,11... | collective-permute-start | bytes 1572872 | tf_op jit(solution)/shard_map/ppermute | solution.py:154
  44.8 1.5 %collective-permute-done.got_ref = f32[512,256]{1,0:T(8,128)S(1)} collective-permute-done((f32[512,256]{1,0:T(8,128)S(1)}, f32[512,256]{1,0:T(8,128)S(1)}, u32[]{:S(2)}, u32[]{:S(2)}) %collective-permute-start) | collective-permute-done | bytes 524320 | tf_op jit(solution)/shard_map/ppermute | solution.py:154
  46.3 0.1 shard_map.120
  46.4 0.0 copy-start.5
  46.4 0.0 copy-start.6
  46.5 19.7 %all_to_all.11.t_ref = bf16[128,8,128]{2,1,0:T(8,128)(2,1)S(1)} all-to-all(bf16[128,8,128]{2,1,0:T(8,128)(2,1)S(1)} %bitcast.6), channel_id=1, replica_groups=mesh['row'=32,'zl'=4,'core'=2] {'row','zl'}, dimensions={0} | all-to-all | bytes 524288 | tf_op jit(solution)/shard_map/all_to_all | solution.py:156
  66.1 0.0 copy-done.5
  66.1 0.0 copy-done.6
  66.1 0.6 copy-done.10
  66.8 0.0 copy-done.11
  66.8 1.4 %shard_map.121 = bf16[16,64,128]{2,1,0:T(8,128)(2,1)} custom-call(bf16[128,8,128]{2,1,0:T(8,128)(2,1)S(1)} %all_to_all.11.t_ref, bf16[16,64,128]{2,1,0:T(8,128)(2,1)S(1)} %get-tuple-element.12.normed_ref, bf16[128,128]{1,0:T(8,128)(2,1)S(1)} %copy-done.5, f32[1,128]{1,0:T(1,128)S(1)} %bitcast.10, f32[1,128]{1,0:T(1,128)S(1)} %bitcast.11, ...), custom_call_target="tpu_custom_call" | custom-call | tf_op jit(solution)/shard_map/pallas_call | solution.py:159
  (8 shorter events, 0.0 us)
Async XLA Ops:
  0.0 0.7 copy-start.7
  0.0 0.7 copy-start.8
  0.0 0.7 %copy-start.9 = (f32[128]{0:T(128)S(1)}, f32[128]{0:T(128)}, u32[]{:S(2)}) copy-start(f32[128]{0:T(128)} %param.15) | copy-start | bytes 1540
  0.7 1.0 %copy-start = (bf16[16,64,128]{2,1,0:T(8,128)(2,1)S(1)}, bf16[16,64,128]{2,1,0:T(8,128)(2,1)}, u32[]{:S(2)}) copy-start(bf16[16,64,128]{2,1,0:T(8,128)(2,1)} %x_ref.1) | copy-start | bytes 786436
  1.6 0.8 %copy-start.1 = (bf16[128,128]{1,0:T(8,128)(2,1)S(1)}, bf16[128,128]{1,0:T(8,128)(2,1)}, u32[]{:S(2)}) copy-start(bf16[128,128]{1,0:T(8,128)(2,1)} %w_l.1) | copy-start | bytes 98308
  2.4 0.8 %copy-start.2 = (bf16[128,128]{1,0:T(8,128)(2,1)S(1)}, bf16[128,128]{1,0:T(8,128)(2,1)}, u32[]{:S(2)}) copy-start(bf16[128,128]{1,0:T(8,128)(2,1)} %w_lg.1) | copy-start | bytes 98308
  3.2 0.8 %copy-start.3 = (bf16[128,128]{1,0:T(8,128)(2,1)S(1)}, bf16[128,128]{1,0:T(8,128)(2,1)}, u32[]{:S(2)}) copy-start(bf16[128,128]{1,0:T(8,128)(2,1)} %w_r.1) | copy-start | bytes 98308
  3.9 0.8 %copy-start.4 = (bf16[128,128]{1,0:T(8,128)(2,1)S(1)}, bf16[128,128]{1,0:T(8,128)(2,1)}, u32[]{:S(2)}) copy-start(bf16[128,128]{1,0:T(8,128)(2,1)} %w_rg.1) | copy-start | bytes 98308
  41.9 4.4 %collective-permute-start = (f32[512,256]{1,0:T(8,128)S(1)}, f32[512,256]{1,0:T(8,128)S(1)}, u32[]{:S(2)}, u32[]{:S(2)}) collective-permute-start(f32[512,256]{1,0:T(8,128)S(1)} %get-tuple-element.11), channel_id=1, source_target_pairs={{0,1},{1,0},{2,3},{3,2},{4,5},{5,4},{6,7},{7,6},{8,9},{9,8},{10,11... | collective-permute-start | bytes 1572872 | tf_op jit(solution)/shard_map/ppermute | solution.py:154
  46.4 19.7 %copy-start.5 = (bf16[128,128]{1,0:T(8,128)(2,1)S(1)}, bf16[128,128]{1,0:T(8,128)(2,1)}, u32[]{:S(2)}) copy-start(bf16[128,128]{1,0:T(8,128)(2,1)} %w_gate.1) | copy-start | bytes 98308
  46.4 19.7 %copy-start.6 = (bf16[128,128]{1,0:T(8,128)(2,1)S(1)}, bf16[128,128]{1,0:T(8,128)(2,1)}, u32[]{:S(2)}) copy-start(bf16[128,128]{1,0:T(8,128)(2,1)} %w_out.1) | copy-start | bytes 98308
  66.1 0.7 copy-start.10
  66.1 0.7 copy-start.11

commit v2 on v1

v2 whole, which is shorter than its diff:
```python
import jax
import jax.numpy as jnp
from jax import lax
from jax.experimental import pallas as pl
from jax.experimental.pallas import tpu as pltpu
from jax.sharding import Mesh, PartitionSpec as P

F32 = jnp.float32
BF16 = jnp.bfloat16
NT = (((1,), (1,)), ((), ()))
TN = (((0,), (0,)), ((), ()))
MIB = 1024 * 1024
VMEM = pl.BlockSpec(memory_space=pltpu.VMEM)
HBM = pl.BlockSpec(memory_space=pltpu.HBM)
PEERS = ("y", "zl", "zh", "x")


def low_lanes(shape):
    return lax.broadcasted_iota(jnp.int32, shape, len(shape) - 1) < 64


def fetch(sources, targets, sems):
    copies = [
        pltpu.make_async_copy(source, target, sems.at[n])
        for n, (source, target) in enumerate(zip(sources, targets))
    ]
    for copy in copies:
        copy.start()
    return copies


def project(
    x_hbm, mask_flat, mask_rows, gain_hbm, bias_hbm, w_l, w_lg, w_r, w_rg,
    out_ref, normed_ref,
    x_ref, mask_scalars, mask_ref, gain, bias, w_ref, rows, sems,
):
    copies = fetch(
        (x_hbm, gain_hbm, bias_hbm, mask_flat, mask_rows, w_l, w_lg, w_r, w_rg),
        (x_ref, gain, bias, mask_scalars, mask_ref) + tuple(w_ref.at[n] for n in range(4)),
        sems,
    )
    row = lax.axis_index("y") * 8 + lax.axis_index("zh") * 4 + lax.axis_index("x")
    core = lax.axis_index("core")
    copies[0].wait()
    x = x_ref[...].astype(F32)
    centred = x - jnp.mean(x, axis=-1, keepdims=True)
    variance = jnp.mean(centred * centred, axis=-1, keepdims=True)
    for copy in copies[1:]:
        copy.wait()
    normed = (centred * lax.rsqrt(variance + 1e-05) * gain[...] + bias[...]).astype(BF16)
    normed_ref[...] = normed
    weights = jnp.concatenate([w_ref[n].T for n in range(4)], axis=0)
    mask_k = mask_ref[pl.ds(lax.axis_index("zl"), 1), :].astype(F32)
    swapped = pltpu.roll(mask_k, 64, 1)
    low = low_lanes((1, 128))
    mask_k = jnp.where(low == (core == 0), mask_k, swapped)
    for s in range(8):
        tokens = jnp.concatenate([normed[s], normed[s + 8]], axis=0)
        p = lax.dot_general(weights, tokens, NT, preferred_element_type=F32)
        mask_a = mask_scalars[row * 16 + s].astype(F32)
        mask_b = mask_scalars[row * 16 + s + 8].astype(F32)
        mask = mask_k * jnp.where(low, mask_a, mask_b)
        left = mask * jax.nn.sigmoid(p[128:256]) * p[:128]
        right = mask * jax.nn.sigmoid(p[384:]) * p[256:384]
        rows[pl.ds(s, 128, stride=16), :] = left
        rows[pl.ds(8 + s, 128, stride=16), :] = right
    out_ref[...] = rows[...].reshape(128, 16, 128).astype(BF16)


def contract(s_ref, keep_ref, send_ref):
    core = lax.axis_index("core")
    edges = s_ref[...].astype(F32).reshape(4, 4, 8, 16, 128)
    low = low_lanes((256, 128))
    left_a, left_b, right, swapped = [], [], [], []
    for z in range(4):
        left_z = edges[:, z, :, :8].reshape(256, 128)
        right_z = edges[:, z, :, 8:].reshape(256, 128)
        left_a.append(jnp.where(low, left_z, 0.0).astype(BF16))
        left_b.append(jnp.where(low, 0.0, left_z).astype(BF16))
        right.append(right_z.astype(BF16))
        swapped.append(pltpu.roll(right_z, 64, 1).astype(BF16))
    left = jnp.concatenate(
        [jnp.concatenate(left_a, axis=1), jnp.concatenate(left_b, axis=1)], axis=0
    )
    right = jnp.concatenate(right, axis=1).reshape(4, 2, 32, 512)
    swapped = jnp.concatenate(swapped, axis=1).reshape(4, 2, 32, 512)
    both = jnp.concatenate([right, swapped], axis=2)
    first, second = both[:, 0].reshape(256, 512), both[:, 1].reshape(256, 512)
    mine = jnp.where(core == 0, first, second)
    other = jnp.where(core == 0, second, first)
    send_ref[...] = lax.dot_general(left, other, NT, preferred_element_type=F32).astype(BF16)
    keep_ref[...] = lax.dot_general(left, mine, NT, preferred_element_type=F32)


def prepare(
    normed_ref, w_gate, w_out_hbm, gain_hbm, bias_hbm,
    gate_ref, w_out_ref, affine_ref,
    w_ref, gain, bias, sems,
):
    copies = fetch(
        (w_gate, w_out_hbm, gain_hbm, bias_hbm), (w_ref, w_out_ref, gain, bias), sems
    )
    for copy in copies:
        copy.wait()
    flat = normed_ref[...].reshape(1024, 128)
    gate = jax.nn.sigmoid(jnp.dot(flat, w_ref[...], preferred_element_type=F32))
    gate_ref[...] = gate.reshape(16, 64, 128)
    affine_ref[0] = jnp.broadcast_to(gain[...], (128, 128)).T
    affine_ref[1] = jnp.broadcast_to(bias[...], (128, 128)).T


def add_halves(keep_ref, got_ref, out_ref):
    low = low_lanes((256, 128))
    for v in range(2):
        cols = slice(128 * v, 128 * v + 128)
        a = keep_ref[:256, cols] + got_ref[:256, cols].astype(F32)
        b = keep_ref[256:, cols] + got_ref[256:, cols].astype(F32)
        even = jnp.where(low, a, pltpu.roll(b, 64, 1))
        odd = jnp.where(low, pltpu.roll(a, 64, 1), b)
        out_ref[:, 2 * v] = even.reshape(4, 8, 8, 128).astype(BF16)
        out_ref[:, 2 * v + 1] = odd.reshape(4, 8, 8, 128).astype(BF16)


def finish(t_ref, gate_ref, w_out, affine, out_hbm, rows, out_ref, sems):
    t = t_ref[...].astype(F32)
    centred = t - jnp.mean(t, axis=0, keepdims=True)
    variance = jnp.mean(centred * centred, axis=0, keepdims=True)
    rows[...] = (centred * lax.rsqrt(variance + 1e-05)).reshape(1024, 128)
    gain_col, bias_col = affine[0], affine[1]
    w = w_out[...]
    copies = []
    for s in range(8):
        n = (rows[pl.ds(s, 128, stride=8), :] * gain_col + bias_col).astype(BF16)
        y = lax.dot_general(n, w, TN, preferred_element_type=F32).reshape(2, 2, 4, 8, 128)
        for b in range(2):
            i = s + 8 * b
            token = jnp.stack([y[b, b], y[b, 1 - b]], axis=1).reshape(64, 128)
            out_ref[i] = (gate_ref[i] * token).astype(BF16)
        if s % 4 == 3:
            for b in range(2):
                part = pl.ds(s - 3 + 8 * b, 4)
                copies.append(
                    pltpu.make_async_copy(
                        out_ref.at[part], out_hbm.at[part], sems.at[len(copies)]
                    )
                )
                copies[-1].start()
    for copy in copies:
        copy.wait()


def call(kernel, outs, specs, scratch=(), out_spec=VMEM, cost=None, limit=24):
    return pl.pallas_call(
        kernel,
        out_shape=outs,
        in_specs=specs,
        out_specs=jax.tree.map(lambda _: out_spec, outs),
        scratch_shapes=scratch,
        compiler_params=pltpu.CompilerParams(vmem_limit_bytes=limit * MIB),
        cost_estimate=cost,
    )


def shape(*dims, dtype=BF16):
    return jax.ShapeDtypeStruct(dims, dtype)


def shards(
    pair,
    token_mask,
    ln_in_gain,
    ln_in_bias,
    w_left,
    w_left_gate,
    w_right,
    w_right_gate,
    w_gate,
    ln_out_gain,
    ln_out_bias,
    w_out,
):
    edges, normed = call(
        project,
        (shape(128, 16, 128), shape(16, 64, 128)),
        [HBM] * 9,
        [
            pltpu.VMEM((16, 64, 128), BF16),
            pltpu.SMEM((512,), jnp.int32),
            pltpu.VMEM((4, 128), jnp.int32),
            pltpu.VMEM((1, 128), F32),
            pltpu.VMEM((1, 128), F32),
            pltpu.VMEM((4, 128, 128), BF16),
            pltpu.VMEM((2048, 128), F32),
            pltpu.SemaphoreType.DMA((9,)),
        ],
        limit=60,
    )(
        pair,
        token_mask,
        token_mask.reshape(4, 128),
        ln_in_gain.reshape(1, 128),
        ln_in_bias.reshape(1, 128),
        w_left,
        w_left_gate,
        w_right,
        w_right_gate,
    )
    edges = lax.all_to_all(edges, PEERS, 0, 0, tiled=True)
    keep, send = call(contract, (shape(512, 256, dtype=F32), shape(512, 256)), [VMEM])(edges)
    got = lax.ppermute(send, "core", [(0, 1), (1, 0)])
    normed, keep = lax.optimization_barrier((normed, keep))
    gate, w_out, affine = call(
        prepare,
        (shape(16, 64, 128, dtype=F32), shape(128, 128), shape(2, 128, 128, dtype=F32)),
        [VMEM] + [HBM] * 4,
        [
            pltpu.VMEM((128, 128), BF16),
            pltpu.VMEM((1, 128), F32),
            pltpu.VMEM((1, 128), F32),
            pltpu.SemaphoreType.DMA((4,)),
        ],
        cost=pl.CostEstimate(
            flops=2 * 1024 * 128 * 128, bytes_accessed=1 << 20, transcendentals=1 << 18
        ),
    )(normed, w_gate, w_out, ln_out_gain.reshape(1, 128), ln_out_bias.reshape(1, 128))
    gate, keep = lax.optimization_barrier((gate, keep))
    triangle = call(add_halves, shape(4, 4, 8, 8, 128), [VMEM] * 2)(keep, got)
    triangle = lax.all_to_all(triangle.reshape(128, 8, 128), PEERS, 0, 0, tiled=True)
    return call(
        finish,
        shape(16, 64, 128),
        [VMEM] * 4,
        [
            pltpu.VMEM((1024, 128), F32),
            pltpu.VMEM((16, 64, 128), BF16),
            pltpu.SemaphoreType.DMA((4,)),
        ],
        out_spec=HBM,
    )(triangle, gate, w_out, affine)


def solution(mesh):
    fine = Mesh(mesh.devices.reshape(4, 2, 4, 4, 2), ("y", "zh", "x", "zl", "core"))
    tile = P(("y", "zh", "x"), ("zl", "core"), None)
    return jax.shard_map(
        shards, mesh=fine, in_specs=(tile,) + (P(),) * 11, out_specs=tile, check_vma=False
    )
```

time: 68.8 us -> 62.2 us (0.904)
  local copies, waits for them, and re-layouts: 5.34 us -> 0.66 us
  blocking collectives: 54.6 us -> 52.2 us
  Pallas kernels: 3.87 us -> 5.24 us
  waiting for transfers between devices: 1.54 us -> 0.17 us
    unnamed x24 -> x10, local copies, waits for them, and re-layouts: 5.34 us -> 0.66 us
    all_to_all x2, blocking collectives: 54.6 us -> 52.2 us  [the longest x1 33.5 us: shards(): edges = lax.all_to_all(edges, PEERS, 0, 0, tiled=True)]
    ppermute x1, waiting for transfers between devices: 1.54 us -> 0.17 us  [shards(): got = lax.ppermute(send, 'core', [(0, 1), (1, 0)])]
    pallas_call x4 -> x5, Pallas kernels: 3.87 us -> 5.24 us  [the longest x1 2.96 us: shards(): call(project, (shape(128, 16, 128), shape(16, 64, 128)), [HBM] * 9, [pltp...]
  transfers between devices with their start and end apart: 1 -> 1, of which waited for: 1 -> 1; matrix products, arithmetic and copies ran while one was open for 0% -> 0% of each run, Pallas kernels for 0% -> 1%
where the time goes in v2:
time: 62.2 us; the launch traced here: 61.2 us
  blocking collectives  52.2 us (84%)
  Pallas kernels  5.24 us (8%)
  starting transfers between devices  2.89 us (5%)
  local copies, waits for them, and re-layouts  0.66 us (1%)
    all_to_all x1, blocking collectives, shards(): edges = lax.all_to_all(edges, PEERS, 0, 0, tiled=True)  33.5 us
    all_to_all x1, blocking collectives, shards(): lax.all_to_all(triangle.reshape(128, 8, 128), PEERS, 0, 0, tiled=True)  18.8 us
    pallas_call x1, Pallas kernels, shards(): call(project, (shape(128, 16, 128), shape(16, 64, 128)), [HBM] * 9, [pltp...  2.96 us
    ppermute x1, starting transfers between devices, shards(): got = lax.ppermute(send, 'core', [(0, 1), (1, 0)])  2.89 us
    pallas_call x1, Pallas kernels, shards(): call(finish, shape(16, 64, 128), [VMEM] * 4, [pltpu.VMEM((1024, 128), F32...  1.3 us
  transfers between devices with their start and end apart: 1, of which 1 were waited for; matrix products, arithmetic and copies ran while one was open for 0% of the time, Pallas kernels for 1%

profile of v2, /device:TPU:1, one launch (start us, length us, event | category | flops | bytes accessed | tf_op | source)
XLA Modules:
  0.0 61.2 jit_solution(8372403277127279551)
XLA Ops:
  0.0 3.0 %shard_map.118 = (bf16[128,16,128]{2,1,0:T(8,128)(2,1)}, bf16[16,64,128]{2,1,0:T(8,128)(2,1)}) custom-call(bf16[16,64,128]{2,1,0:T(8,128)(2,1)} %x_hbm.1, s32[512]{0:T(512)} %mask_flat.1, s32[4,128]{1,0:T(4,128)} %bitcast.9, f32[1,128]{1,0:T(1,128)} %bitcast.10, f32[1,128]{1,0:T(1,128)} %bitcast.11, bf16[128,128]{1,0:T(8,128)(2,1)} %w_l.1, ...), custom_call_target="tpu_custom_call" | custom-call | tf_op jit(solution)/shard_map/pallas_call | solution.py:182
  3.0 33.5 %all_to_all.10.s_ref = bf16[128,16,128]{2,1,0:T(8,128)(2,1)S(1)} all-to-all(bf16[128,16,128]{2,1,0:T(8,128)(2,1)} %get-tuple-element.17), channel_id=1, replica_groups=mesh['y'=4,'zh'=2,'x'=4,'zl'=4,'core'=2] {'y','zl','zh','x'}, dimensions={0} | all-to-all | bytes 1048576 | tf_op jit(solution)/shard_map/all_to_all | solution.py:208
  36.4 0.0 copy-start
  36.4 0.0 copy-start.1
  36.4 0.0 copy-start.2
  36.4 0.5 shard_map.119
  37.0 2.9 %collective-permute-start = (bf16[512,256]{1,0:T(8,128)(2,1)S(1)}, bf16[512,256]{1,0:T(8,128)(2,1)S(1)}, u32[]{:S(2)}, u32[]{:S(2)}) collective-permute-start(bf16[512,256]{1,0:T(8,128)(2,1)S(1)} %get-tuple-element.23), channel_id=1, source_target_pairs={{0,1},{1,0},{2,3},{3,2},{4,5},{5,4},{6,7},{7,6},{8,9},{9,8},{10,11... | collective-permute-start | bytes 786440 | tf_op jit(solution)/shard_map/ppermute | solution.py:210
  39.9 0.0 copy-start.3
  39.9 0.0 copy-start.4
  39.9 0.0 copy-done
  39.9 0.0 copy-done.1
  39.9 0.0 copy-done.2
  39.9 0.6 %copy-done.3 = f32[128]{0:T(128)S(1)} copy-done((f32[128]{0:T(128)S(1)}, f32[128]{0:T(128)}, u32[]{:S(2)}) %copy-start.3) | copy-done | bytes 536
  40.5 0.0 copy-done.4
  40.5 0.3 shard_map.120
  40.9 0.2 collective-permute-done.got_ref
  41.0 0.1 shard_map.121
  41.2 18.8 %all_to_all.11.t_ref = bf16[128,8,128]{2,1,0:T(8,128)(2,1)S(1)} all-to-all(bf16[128,8,128]{2,1,0:T(8,128)(2,1)S(1)} %bitcast.6), channel_id=1, replica_groups=mesh['y'=4,'zh'=2,'x'=4,'zl'=4,'core'=2] {'y','zl','zh','x'}, dimensions={0} | all-to-all | bytes 524288 | tf_op jit(solution)/shard_map/all_to_all | solution.py:228
  60.0 1.3 %shard_map.122 = bf16[16,64,128]{2,1,0:T(8,128)(2,1)} custom-call(bf16[128,8,128]{2,1,0:T(8,128)(2,1)S(1)} %all_to_all.11.t_ref, f32[16,64,128]{2,1,0:T(8,128)S(1)} %get-tuple-element.24.gate_ref, bf16[128,128]{1,0:T(8,128)(2,1)S(1)} %get-tuple-element.25.w_out, f32[2,128,128]{2,1,0:T(8,128)S(1)} %get-tuple-element.26.affine), custom_call_target="tpu_custom_call" | custom-call | tf_op jit(solution)/shard_map/pallas_call | solution.py:229
Async XLA Ops:
  36.4 3.4 %copy-start = (bf16[16,64,128]{2,1,0:T(8,128)(2,1)S(1)}, bf16[16,64,128]{2,1,0:T(8,128)(2,1)}, u32[]{:S(2)}) copy-start(bf16[16,64,128]{2,1,0:T(8,128)(2,1)} %get-tuple-element.19.normed_ref) | copy-start | bytes 786436
  36.4 3.4 %copy-start.1 = (bf16[128,128]{1,0:T(8,128)(2,1)S(1)}, bf16[128,128]{1,0:T(8,128)(2,1)}, u32[]{:S(2)}) copy-start(bf16[128,128]{1,0:T(8,128)(2,1)} %w_gate.1) | copy-start | bytes 98308
  36.4 3.4 %copy-start.2 = (bf16[128,128]{1,0:T(8,128)(2,1)S(1)}, bf16[128,128]{1,0:T(8,128)(2,1)}, u32[]{:S(2)}) copy-start(bf16[128,128]{1,0:T(8,128)(2,1)} %w_out_hbm.1) | copy-start | bytes 98308
  37.0 4.0 %collective-permute-start = (bf16[512,256]{1,0:T(8,128)(2,1)S(1)}, bf16[512,256]{1,0:T(8,128)(2,1)S(1)}, u32[]{:S(2)}, u32[]{:S(2)}) collective-permute-start(bf16[512,256]{1,0:T(8,128)(2,1)S(1)} %get-tuple-element.23), channel_id=1, source_target_pairs={{0,1},{1,0},{2,3},{3,2},{4,5},{5,4},{6,7},{7,6},{8,9},{9,8},{10,11... | collective-permute-start | bytes 786440 | tf_op jit(solution)/shard_map/ppermute | solution.py:210
  39.9 0.7 %copy-start.3 = (f32[128]{0:T(128)S(1)}, f32[128]{0:T(128)}, u32[]{:S(2)}) copy-start(f32[128]{0:T(128)} %param.21) | copy-start | bytes 1540
  39.9 0.7 %copy-start.4 = (f32[128]{0:T(128)S(1)}, f32[128]{0:T(128)}, u32[]{:S(2)}) copy-start(f32[128]{0:T(128)} %param.22) | copy-start | bytes 1540

commit v3 on v2

--- a/solution.py
+++ b/solution.py
@@ -12,7 +12,7 @@
 MIB = 1024 * 1024
 VMEM = pl.BlockSpec(memory_space=pltpu.VMEM)
 HBM = pl.BlockSpec(memory_space=pltpu.HBM)
-PEERS = ("y", "zl", "zh", "x")
+PEERS = ("zl", "zh", "y", "x")
 
 
 def low_lanes(shape):
@@ -69,12 +69,13 @@
 
 def contract(s_ref, keep_ref, send_ref):
     core = lax.axis_index("core")
-    edges = s_ref[...].astype(F32).reshape(4, 4, 8, 16, 128)
+    edges = s_ref[...].astype(F32).reshape(4, 2, 4, 4, 16, 128)
+    edges = jnp.stack([edges[:, 0], edges[:, 1]], axis=2).reshape(4, 32, 16, 128)
     low = low_lanes((256, 128))
     left_a, left_b, right, swapped = [], [], [], []
     for z in range(4):
-        left_z = edges[:, z, :, :8].reshape(256, 128)
-        right_z = edges[:, z, :, 8:].reshape(256, 128)
+        left_z = edges[z, :, :8].reshape(256, 128)
+        right_z = edges[z, :, 8:].reshape(256, 128)
         left_a.append(jnp.where(low, left_z, 0.0).astype(BF16))
         left_b.append(jnp.where(low, 0.0, left_z).astype(BF16))
         right.append(right_z.astype(BF16))
@@ -117,8 +118,11 @@
         b = keep_ref[256:, cols] + got_ref[256:, cols].astype(F32)
         even = jnp.where(low, a, pltpu.roll(b, 64, 1))
         odd = jnp.where(low, pltpu.roll(a, 64, 1), b)
-        out_ref[:, 2 * v] = even.reshape(4, 8, 8, 128).astype(BF16)
-        out_ref[:, 2 * v + 1] = odd.reshape(4, 8, 8, 128).astype(BF16)
+        even = even.reshape(4, 2, 4, 8, 128).astype(BF16)
+        odd = odd.reshape(4, 2, 4, 8, 128).astype(BF16)
+        for zh in range(2):
+            out_ref[2 * v, zh] = even[:, zh]
+            out_ref[2 * v + 1, zh] = odd[:, zh]
 
 
 def finish(t_ref, gate_ref, w_out, affine, out_hbm, rows, out_ref, sems):
@@ -161,6 +165,10 @@
     )
 
 
+def in_hbm(*arrays):
+    return [pltpu.with_memory_space_constraint(a, pltpu.HBM) for a in arrays]
+
+
 def shape(*dims, dtype=BF16):
     return jax.ShapeDtypeStruct(dims, dtype)
 
@@ -193,17 +201,18 @@
             pltpu.VMEM((2048, 128), F32),
             pltpu.SemaphoreType.DMA((9,)),
         ],
-        limit=60,
     )(
-        pair,
-        token_mask,
-        token_mask.reshape(4, 128),
-        ln_in_gain.reshape(1, 128),
-        ln_in_bias.reshape(1, 128),
-        w_left,
-        w_left_gate,
-        w_right,
-        w_right_gate,
+        *in_hbm(
+            pair,
+            token_mask,
+            token_mask.reshape(4, 128),
+            ln_in_gain.reshape(1, 128),
+            ln_in_bias.reshape(1, 128),
+            w_left,
+            w_left_gate,
+            w_right,
+            w_right_gate,
+        )
     )
     edges = lax.all_to_all(edges, PEERS, 0, 0, tiled=True)
     keep, send = call(contract, (shape(512, 256, dtype=F32), shape(512, 256)), [VMEM])(edges)
@@ -222,9 +231,12 @@
         cost=pl.CostEstimate(
             flops=2 * 1024 * 128 * 128, bytes_accessed=1 << 20, transcendentals=1 << 18
         ),
-    )(normed, w_gate, w_out, ln_out_gain.reshape(1, 128), ln_out_bias.reshape(1, 128))
+    )(
+        normed,
+        *in_hbm(w_gate, w_out, ln_out_gain.reshape(1, 128), ln_out_bias.reshape(1, 128)),
+    )
     gate, keep = lax.optimization_barrier((gate, keep))
-    triangle = call(add_halves, shape(4, 4, 8, 8, 128), [VMEM] * 2)(keep, got)
+    triangle = call(add_halves, shape(4, 2, 4, 4, 8, 128), [VMEM] * 2)(keep, got)
     triangle = lax.all_to_all(triangle.reshape(128, 8, 128), PEERS, 0, 0, tiled=True)
     return call(
         finish,

time: 62.2 us -> 60.4 us (0.971)
  blocking collectives: 52.2 us -> 51 us
  local copies, waits for them, and re-layouts: 0.66 us -> 0 us
    all_to_all x1, blocking collectives: 33.5 us -> 32.3 us  [shards(): edges = lax.all_to_all(edges, PEERS, 0, 0, tiled=True)]
    pallas_call x1, Pallas kernels: 2.96 us -> 2.15 us  [shards(): call(project, (shape(128, 16, 128), shape(16, 64, 128)), [HBM] * 9, [pltp...]
    pallas_call x1, Pallas kernels: 0.31 us -> 1.04 us  [shards(): call(prepare, (shape(16, 64, 128, dtype=F32), shape(128, 128), shape(2, 1...]
    unnamed x10 -> x0, local copies, waits for them, and re-layouts: 0.66 us -> none
  transfers between devices with their start and end apart: 1 -> 1, of which waited for: 1 -> 1; matrix products, arithmetic and copies ran while one was open for 0% -> 0% of each run, Pallas kernels for 1% -> 2%
where the time goes in v3:
time: 60.4 us; the launch traced here: 59.6 us
  blocking collectives  51 us (84%)
  Pallas kernels  5.16 us (9%)
  starting transfers between devices  3.33 us (6%)
    all_to_all x1, blocking collectives, shards(): edges = lax.all_to_all(edges, PEERS, 0, 0, tiled=True)  32.3 us
    all_to_all x1, blocking collectives, shards(): lax.all_to_all(triangle.reshape(128, 8, 128), PEERS, 0, 0, tiled=True)  18.7 us
    ppermute x1, starting transfers between devices, shards(): got = lax.ppermute(send, 'core', [(0, 1), (1, 0)])  3.33 us
    pallas_call x1, Pallas kernels, shards(): call(project, (shape(128, 16, 128), shape(16, 64, 128)), [HBM] * 9, [pltp...  2.15 us
    pallas_call x1, Pallas kernels, shards(): call(finish, shape(16, 64, 128), [VMEM] * 4, [pltpu.VMEM((1024, 128), F32...  1.29 us
  transfers between devices with their start and end apart: 1, of which 1 were waited for; matrix products, arithmetic and copies ran while one was open for 0% of the time, Pallas kernels for 2%

profile of v3, /device:TPU:1, one launch (start us, length us, event | category | flops | bytes accessed | tf_op | source)
XLA Modules:
  0.0 59.6 jit_solution(2985611911093215138)
XLA Ops:
  0.0 2.2 %shard_map.118 = (bf16[128,16,128]{2,1,0:T(8,128)(2,1)S(1)}, bf16[16,64,128]{2,1,0:T(8,128)(2,1)S(1)}) custom-call(bf16[16,64,128]{2,1,0:T(8,128)(2,1)} %x_hbm.1, s32[512]{0:T(512)} %mask_flat.1, s32[4,128]{1,0:T(4,128)} %bitcast.7, f32[1,128]{1,0:T(1,128)} %bitcast.8, f32[1,128]{1,0:T(1,128)} %bitcast.9, bf16[128,128]{1,0:T(8,128)(2,1)} %w_l.1, ...), custom_call_target="tpu_custom_call" | custom-call | tf_op jit(solution)/shard_map/pallas_call | solution.py:190
  2.2 32.3 %all_to_all.10.s_ref = bf16[128,16,128]{2,1,0:T(8,128)(2,1)S(1)} all-to-all(bf16[128,16,128]{2,1,0:T(8,128)(2,1)S(1)} %get-tuple-element.17), channel_id=1, replica_groups=mesh['y'=4,'zh'=2,'x'=4,'zl'=4,'core'=2] {'zl','zh','y','x'}, dimensions={0} | all-to-all | bytes 1048576 | tf_op jit(solution)/shard_map/all_to_all | solution.py:217
  34.4 0.5 shard_map.119
  35.0 3.3 %collective-permute-start = (bf16[512,256]{1,0:T(8,128)(2,1)S(1)}, bf16[512,256]{1,0:T(8,128)(2,1)S(1)}, u32[]{:S(2)}, u32[]{:S(2)}) collective-permute-start(bf16[512,256]{1,0:T(8,128)(2,1)S(1)} %get-tuple-element.23), channel_id=1, source_target_pairs={{0,1},{1,0},{2,3},{3,2},{4,5},{5,4},{6,7},{7,6},{8,9},{9,8},{10,11... | collective-permute-start | bytes 786440 | tf_op jit(solution)/shard_map/ppermute | solution.py:219
  38.3 1.0 %shard_map.120 = (f32[16,64,128]{2,1,0:T(8,128)S(1)}, bf16[128,128]{1,0:T(8,128)(2,1)S(1)}, f32[2,128,128]{2,1,0:T(8,128)S(1)}) custom-call(bf16[16,64,128]{2,1,0:T(8,128)(2,1)S(1)} %get-tuple-element.19.normed_ref, bf16[128,128]{1,0:T(8,128)(2,1)} %w_gate.1, bf16[128,128]{1,0:T(8,128)(2,1)} %w_out_hbm.1, f32[1,128]{1,0:T(1,128)} %bitcast.10, f32[1,128]{1,0:T(1,128)} %bitcast.11), custom_call_target="tpu_custom_call" | custom-call | flops 33554432 | bytes 1048576 | tf_op jit(solution)/shard_map/pallas_call | solution.py:221
  39.3 0.1 collective-permute-done.got_ref
  39.5 0.1 shard_map.121
  39.6 18.7 %all_to_all.11.t_ref = bf16[128,8,128]{2,1,0:T(8,128)(2,1)S(1)} all-to-all(bf16[128,8,128]{2,1,0:T(8,128)(2,1)S(1)} %bitcast.6), channel_id=1, replica_groups=mesh['y'=4,'zh'=2,'x'=4,'zl'=4,'core'=2] {'zl','zh','y','x'}, dimensions={0} | all-to-all | bytes 524288 | tf_op jit(solution)/shard_map/all_to_all | solution.py:240
  58.3 1.3 %shard_map.122 = bf16[16,64,128]{2,1,0:T(8,128)(2,1)} custom-call(bf16[128,8,128]{2,1,0:T(8,128)(2,1)S(1)} %all_to_all.11.t_ref, f32[16,64,128]{2,1,0:T(8,128)S(1)} %get-tuple-element.24.gate_ref, bf16[128,128]{1,0:T(8,128)(2,1)S(1)} %get-tuple-element.25.w_out, f32[2,128,128]{2,1,0:T(8,128)S(1)} %get-tuple-element.26.affine), custom_call_target="tpu_custom_call" | custom-call | tf_op jit(solution)/shard_map/pallas_call | solution.py:241
Async XLA Ops:
  35.0 4.5 %collective-permute-start = (bf16[512,256]{1,0:T(8,128)(2,1)S(1)}, bf16[512,256]{1,0:T(8,128)(2,1)S(1)}, u32[]{:S(2)}, u32[]{:S(2)}) collective-permute-start(bf16[512,256]{1,0:T(8,128)(2,1)S(1)} %get-tuple-element.23), channel_id=1, source_target_pairs={{0,1},{1,0},{2,3},{3,2},{4,5},{5,4},{6,7},{7,6},{8,9},{9,8},{10,11... | collective-permute-start | bytes 786440 | tf_op jit(solution)/shard_map/ppermute | solution.py:219

commit v4 on v3

--- a/solution.py
+++ b/solution.py
@@ -54,17 +54,17 @@
     swapped = pltpu.roll(mask_k, 64, 1)
     low = low_lanes((1, 128))
     mask_k = jnp.where(low == (core == 0), mask_k, swapped)
+    pall = lax.dot_general(weights, jnp.concatenate([normed[(s//2)+8*(s%2)] for s in range(16)],axis=0), NT, preferred_element_type=F32)
     for s in range(8):
-        tokens = jnp.concatenate([normed[s], normed[s + 8]], axis=0)
-        p = lax.dot_general(weights, tokens, NT, preferred_element_type=F32)
+        p = pall[:, 128*s:128*s+128]
         mask_a = mask_scalars[row * 16 + s].astype(F32)
         mask_b = mask_scalars[row * 16 + s + 8].astype(F32)
         mask = mask_k * jnp.where(low, mask_a, mask_b)
         left = mask * jax.nn.sigmoid(p[128:256]) * p[:128]
         right = mask * jax.nn.sigmoid(p[384:]) * p[256:384]
-        rows[pl.ds(s, 128, stride=16), :] = left
-        rows[pl.ds(8 + s, 128, stride=16), :] = right
-    out_ref[...] = rows[...].reshape(128, 16, 128).astype(BF16)
+        rows[pl.ds(s, 128, stride=8), :] = left
+        rows[pl.ds(1024 + s, 128, stride=8), :] = right
+    out_ref[...] = jnp.concatenate([rows[:1024].reshape(128,8,128), rows[1024:].reshape(128,8,128)],axis=1).astype(BF16)
 
 
 def contract(s_ref, keep_ref, send_ref):
@@ -72,21 +72,18 @@
     edges = s_ref[...].astype(F32).reshape(4, 2, 4, 4, 16, 128)
     edges = jnp.stack([edges[:, 0], edges[:, 1]], axis=2).reshape(4, 32, 16, 128)
     low = low_lanes((256, 128))
-    left_a, left_b, right, swapped = [], [], [], []
-    for z in range(4):
-        left_z = edges[z, :, :8].reshape(256, 128)
-        right_z = edges[z, :, 8:].reshape(256, 128)
-        left_a.append(jnp.where(low, left_z, 0.0).astype(BF16))
-        left_b.append(jnp.where(low, 0.0, left_z).astype(BF16))
-        right.append(right_z.astype(BF16))
-        swapped.append(pltpu.roll(right_z, 64, 1).astype(BF16))
-    left = jnp.concatenate(
-        [jnp.concatenate(left_a, axis=1), jnp.concatenate(left_b, axis=1)], axis=0
-    )
-    right = jnp.concatenate(right, axis=1).reshape(4, 2, 32, 512)
-    swapped = jnp.concatenate(swapped, axis=1).reshape(4, 2, 32, 512)
-    both = jnp.concatenate([right, swapped], axis=2)
-    first, second = both[:, 0].reshape(256, 512), both[:, 1].reshape(256, 512)
+    def halves(part):
+        first, second = [], []
+        for z in (0, 2):
+            a, b = part(z), part(z + 1)
+            first.append(jnp.where(low, a, pltpu.roll(b, 64, 1)).astype(BF16))
+            second.append(jnp.where(low, pltpu.roll(a, 64, 1), b).astype(BF16))
+        return jnp.concatenate(first, axis=1), jnp.concatenate(second, axis=1)
+
+    left = jnp.concatenate(halves(lambda z: edges[z, :, :8].reshape(256, 128)), axis=0)
+    right = halves(lambda z: edges[z, :, 8:].reshape(256, 128))
+    both = jnp.concatenate([r.reshape(4, 2, 32, 256) for r in right], axis=2)
+    first, second = both[:, 0].reshape(256, 256), both[:, 1].reshape(256, 256)
     mine = jnp.where(core == 0, first, second)
     other = jnp.where(core == 0, second, first)
     send_ref[...] = lax.dot_general(left, other, NT, preferred_element_type=F32).astype(BF16)
@@ -138,7 +135,7 @@
         y = lax.dot_general(n, w, TN, preferred_element_type=F32).reshape(2, 2, 4, 8, 128)
         for b in range(2):
             i = s + 8 * b
-            token = jnp.stack([y[b, b], y[b, 1 - b]], axis=1).reshape(64, 128)
+            token = jnp.stack([y[b, 0], y[b, 1]], axis=1).reshape(64, 128)
             out_ref[i] = (gate_ref[i] * token).astype(BF16)
         if s % 4 == 3:
             for b in range(2):

time: 60.4 us -> 60.2 us (level)
  no operation moved by 1% of the time
where the time goes in v4:
time: 60.2 us; the launch traced here: 59.3 us
  blocking collectives  50.9 us (85%)
  Pallas kernels  4.88 us (8%)
  starting transfers between devices  3.34 us (6%)
    all_to_all x1, blocking collectives, shards(): edges = lax.all_to_all(edges, PEERS, 0, 0, tiled=True)  32.3 us
    all_to_all x1, blocking collectives, shards(): lax.all_to_all(triangle.reshape(128, 8, 128), PEERS, 0, 0, tiled=True)  18.7 us
    ppermute x1, starting transfers between devices, shards(): got = lax.ppermute(send, 'core', [(0, 1), (1, 0)])  3.34 us
    pallas_call x1, Pallas kernels, shards(): call(project, (shape(128, 16, 128), shape(16, 64, 128)), [HBM] * 9, [pltp...  1.97 us
    pallas_call x1, Pallas kernels, shards(): call(finish, shape(16, 64, 128), [VMEM] * 4, [pltpu.VMEM((1024, 128), F32...  1.29 us
  transfers between devices with their start and end apart: 1, of which 1 were waited for; matrix products, arithmetic and copies ran while one was open for 0% of the time, Pallas kernels for 2%

profile of v4, /device:TPU:1, one launch (start us, length us, event | category | flops | bytes accessed | tf_op | source)
XLA Modules:
  0.0 59.3 jit_solution(609243573301347362)
XLA Ops:
  0.0 2.0 %shard_map.118 = (bf16[128,16,128]{2,1,0:T(8,128)(2,1)S(1)}, bf16[16,64,128]{2,1,0:T(8,128)(2,1)S(1)}) custom-call(bf16[16,64,128]{2,1,0:T(8,128)(2,1)} %x_hbm.1, s32[512]{0:T(512)} %mask_flat.1, s32[4,128]{1,0:T(4,128)} %bitcast.7, f32[1,128]{1,0:T(1,128)} %bitcast.8, f32[1,128]{1,0:T(1,128)} %bitcast.9, bf16[128,128]{1,0:T(8,128)(2,1)} %w_l.1, ...), custom_call_target="tpu_custom_call" | custom-call | tf_op jit(solution)/shard_map/pallas_call | solution.py:187
  2.0 32.3 %all_to_all.10.s_ref = bf16[128,16,128]{2,1,0:T(8,128)(2,1)S(1)} all-to-all(bf16[128,16,128]{2,1,0:T(8,128)(2,1)S(1)} %get-tuple-element.17), channel_id=1, replica_groups=mesh['y'=4,'zh'=2,'x'=4,'zl'=4,'core'=2] {'zl','zh','y','x'}, dimensions={0} | all-to-all | bytes 1048576 | tf_op jit(solution)/shard_map/all_to_all | solution.py:214
  34.2 0.5 shard_map.119
  34.7 3.3 %collective-permute-start = (bf16[512,256]{1,0:T(8,128)(2,1)S(1)}, bf16[512,256]{1,0:T(8,128)(2,1)S(1)}, u32[]{:S(2)}, u32[]{:S(2)}) collective-permute-start(bf16[512,256]{1,0:T(8,128)(2,1)S(1)} %get-tuple-element.23), channel_id=1, source_target_pairs={{0,1},{1,0},{2,3},{3,2},{4,5},{5,4},{6,7},{7,6},{8,9},{9,8},{10,11... | collective-permute-start | bytes 786440 | tf_op jit(solution)/shard_map/ppermute | solution.py:216
  38.0 1.0 %shard_map.120 = (f32[16,64,128]{2,1,0:T(8,128)S(1)}, bf16[128,128]{1,0:T(8,128)(2,1)S(1)}, f32[2,128,128]{2,1,0:T(8,128)S(1)}) custom-call(bf16[16,64,128]{2,1,0:T(8,128)(2,1)S(1)} %get-tuple-element.19.normed_ref, bf16[128,128]{1,0:T(8,128)(2,1)} %w_gate.1, bf16[128,128]{1,0:T(8,128)(2,1)} %w_out_hbm.1, f32[1,128]{1,0:T(1,128)} %bitcast.10, f32[1,128]{1,0:T(1,128)} %bitcast.11), custom_call_target="tpu_custom_call" | custom-call | flops 33554432 | bytes 1048576 | tf_op jit(solution)/shard_map/pallas_call | solution.py:218
  39.1 0.1 collective-permute-done.got_ref
  39.2 0.1 shard_map.121
  39.3 18.7 %all_to_all.11.t_ref = bf16[128,8,128]{2,1,0:T(8,128)(2,1)S(1)} all-to-all(bf16[128,8,128]{2,1,0:T(8,128)(2,1)S(1)} %bitcast.6), channel_id=1, replica_groups=mesh['y'=4,'zh'=2,'x'=4,'zl'=4,'core'=2] {'zl','zh','y','x'}, dimensions={0} | all-to-all | bytes 524288 | tf_op jit(solution)/shard_map/all_to_all | solution.py:237
  58.0 1.3 %shard_map.122 = bf16[16,64,128]{2,1,0:T(8,128)(2,1)} custom-call(bf16[128,8,128]{2,1,0:T(8,128)(2,1)S(1)} %all_to_all.11.t_ref, f32[16,64,128]{2,1,0:T(8,128)S(1)} %get-tuple-element.24.gate_ref, bf16[128,128]{1,0:T(8,128)(2,1)S(1)} %get-tuple-element.25.w_out, f32[2,128,128]{2,1,0:T(8,128)S(1)} %get-tuple-element.26.affine), custom_call_target="tpu_custom_call" | custom-call | tf_op jit(solution)/shard_map/pallas_call | solution.py:238
Async XLA Ops:
  34.7 4.5 %collective-permute-start = (bf16[512,256]{1,0:T(8,128)(2,1)S(1)}, bf16[512,256]{1,0:T(8,128)(2,1)S(1)}, u32[]{:S(2)}, u32[]{:S(2)}) collective-permute-start(bf16[512,256]{1,0:T(8,128)(2,1)S(1)} %get-tuple-element.23), channel_id=1, source_target_pairs={{0,1},{1,0},{2,3},{3,2},{4,5},{5,4},{6,7},{7,6},{8,9},{9,8},{10,11... | collective-permute-start | bytes 786440 | tf_op jit(solution)/shard_map/ppermute | solution.py:216

commit v5 on v4

--- a/solution.py
+++ b/solution.py
@@ -41,29 +41,34 @@
     )
     row = lax.axis_index("y") * 8 + lax.axis_index("zh") * 4 + lax.axis_index("x")
     core = lax.axis_index("core")
-    copies[0].wait()
-    x = x_ref[...].astype(F32)
-    centred = x - jnp.mean(x, axis=-1, keepdims=True)
-    variance = jnp.mean(centred * centred, axis=-1, keepdims=True)
-    for copy in copies[1:]:
+    for copy in copies:
         copy.wait()
-    normed = (centred * lax.rsqrt(variance + 1e-05) * gain[...] + bias[...]).astype(BF16)
-    normed_ref[...] = normed
     weights = jnp.concatenate([w_ref[n].T for n in range(4)], axis=0)
     mask_k = mask_ref[pl.ds(lax.axis_index("zl"), 1), :].astype(F32)
     swapped = pltpu.roll(mask_k, 64, 1)
     low = low_lanes((1, 128))
     mask_k = jnp.where(low == (core == 0), mask_k, swapped)
-    pall = lax.dot_general(weights, jnp.concatenate([normed[(s//2)+8*(s%2)] for s in range(16)],axis=0), NT, preferred_element_type=F32)
-    for s in range(8):
-        p = pall[:, 128*s:128*s+128]
-        mask_a = mask_scalars[row * 16 + s].astype(F32)
-        mask_b = mask_scalars[row * 16 + s + 8].astype(F32)
-        mask = mask_k * jnp.where(low, mask_a, mask_b)
-        left = mask * jax.nn.sigmoid(p[128:256]) * p[:128]
-        right = mask * jax.nn.sigmoid(p[384:]) * p[256:384]
-        rows[pl.ds(s, 128, stride=8), :] = left
-        rows[pl.ds(1024 + s, 128, stride=8), :] = right
+    for first in range(0, 8, 2):
+        parts = []
+        for start in (first, first + 8):
+            x = x_ref[start : start + 2].astype(F32)
+            centred = x - jnp.mean(x, axis=-1, keepdims=True)
+            variance = jnp.mean(centred * centred, axis=-1, keepdims=True)
+            part = centred * lax.rsqrt(variance + 1e-05) * gain[...] + bias[...]
+            parts.append(part.astype(BF16))
+            normed_ref[start : start + 2] = parts[-1]
+        tokens = jnp.stack(parts, axis=1).reshape(128 * 2, 128)
+        projected = lax.dot_general(weights, tokens, NT, preferred_element_type=F32)
+        for n in range(2):
+            s = first + n
+            p = projected[:, 128 * n : 128 * n + 128]
+            mask_a = mask_scalars[row * 16 + s].astype(F32)
+            mask_b = mask_scalars[row * 16 + s + 8].astype(F32)
+            mask = mask_k * jnp.where(low, mask_a, mask_b)
+            left = mask * jax.nn.sigmoid(p[128:256]) * p[:128]
+            right = mask * jax.nn.sigmoid(p[384:]) * p[256:384]
+            rows[pl.ds(s, 128, stride=8), :] = left
+            rows[pl.ds(1024 + s, 128, stride=8), :] = right
     out_ref[...] = jnp.concatenate([rows[:1024].reshape(128,8,128), rows[1024:].reshape(128,8,128)],axis=1).astype(BF16)
 
 
@@ -124,14 +129,15 @@
 
 def finish(t_ref, gate_ref, w_out, affine, out_hbm, rows, out_ref, sems):
     t = t_ref[...].astype(F32)
-    centred = t - jnp.mean(t, axis=0, keepdims=True)
-    variance = jnp.mean(centred * centred, axis=0, keepdims=True)
-    rows[...] = (centred * lax.rsqrt(variance + 1e-05)).reshape(1024, 128)
+    rows[...] = t.reshape(1024, 128)
     gain_col, bias_col = affine[0], affine[1]
     w = w_out[...]
     copies = []
     for s in range(8):
-        n = (rows[pl.ds(s, 128, stride=8), :] * gain_col + bias_col).astype(BF16)
+        n = rows[pl.ds(s, 128, stride=8), :]
+        n = n - jnp.mean(n, axis=0, keepdims=True)
+        variance = jnp.mean(n * n, axis=0, keepdims=True)
+        n = (n * lax.rsqrt(variance + 1e-05) * gain_col + bias_col).astype(BF16)
         y = lax.dot_general(n, w, TN, preferred_element_type=F32).reshape(2, 2, 4, 8, 128)
         for b in range(2):
             i = s + 8 * b

time: 60.2 us -> 59.9 us (level)
  no operation moved by 1% of the time
where the time goes in v5:
time: 59.9 us; the launch traced here: 59.1 us
  blocking collectives  51 us (85%)
  Pallas kernels  4.66 us (8%)
  starting transfers between devices  3.32 us (6%)
    all_to_all x1, blocking collectives, shards(): edges = lax.all_to_all(edges, PEERS, 0, 0, tiled=True)  32.3 us
    all_to_all x1, blocking collectives, shards(): lax.all_to_all(triangle.reshape(128, 8, 128), PEERS, 0, 0, tiled=True)  18.7 us
    ppermute x1, starting transfers between devices, shards(): got = lax.ppermute(send, 'core', [(0, 1), (1, 0)])  3.32 us
    pallas_call x1, Pallas kernels, shards(): call(project, (shape(128, 16, 128), shape(16, 64, 128)), [HBM] * 9, [pltp...  1.9 us
  transfers between devices with their start and end apart: 1, of which 1 were waited for; matrix products, arithmetic and copies ran while one was open for 0% of the time, Pallas kernels for 2%

profile of v5, /device:TPU:1, one launch (start us, length us, event | category | flops | bytes accessed | tf_op | source)
XLA Modules:
  0.0 59.1 jit_solution(14231506769817979945)
XLA Ops:
  0.0 1.9 %shard_map.118 = (bf16[128,16,128]{2,1,0:T(8,128)(2,1)S(1)}, bf16[16,64,128]{2,1,0:T(8,128)(2,1)S(1)}) custom-call(bf16[16,64,128]{2,1,0:T(8,128)(2,1)} %x_hbm.1, s32[512]{0:T(512)} %mask_flat.1, s32[4,128]{1,0:T(4,128)} %bitcast.7, f32[1,128]{1,0:T(1,128)} %bitcast.8, f32[1,128]{1,0:T(1,128)} %bitcast.9, bf16[128,128]{1,0:T(8,128)(2,1)} %w_l.1, ...), custom_call_target="tpu_custom_call" | custom-call | tf_op jit(solution)/shard_map/pallas_call | solution.py:193
  1.9 32.3 %all_to_all.10.s_ref = bf16[128,16,128]{2,1,0:T(8,128)(2,1)S(1)} all-to-all(bf16[128,16,128]{2,1,0:T(8,128)(2,1)S(1)} %get-tuple-element.17), channel_id=1, replica_groups=mesh['y'=4,'zh'=2,'x'=4,'zl'=4,'core'=2] {'zl','zh','y','x'}, dimensions={0} | all-to-all | bytes 1048576 | tf_op jit(solution)/shard_map/all_to_all | solution.py:220
  34.2 0.5 shard_map.119
  34.6 3.3 %collective-permute-start = (bf16[512,256]{1,0:T(8,128)(2,1)S(1)}, bf16[512,256]{1,0:T(8,128)(2,1)S(1)}, u32[]{:S(2)}, u32[]{:S(2)}) collective-permute-start(bf16[512,256]{1,0:T(8,128)(2,1)S(1)} %get-tuple-element.23), channel_id=1, source_target_pairs={{0,1},{1,0},{2,3},{3,2},{4,5},{5,4},{6,7},{7,6},{8,9},{9,8},{10,11... | collective-permute-start | bytes 786440 | tf_op jit(solution)/shard_map/ppermute | solution.py:222
  38.0 1.0 %shard_map.120 = (f32[16,64,128]{2,1,0:T(8,128)S(1)}, bf16[128,128]{1,0:T(8,128)(2,1)S(1)}, f32[2,128,128]{2,1,0:T(8,128)S(1)}) custom-call(bf16[16,64,128]{2,1,0:T(8,128)(2,1)S(1)} %get-tuple-element.19.normed_ref, bf16[128,128]{1,0:T(8,128)(2,1)} %w_gate.1, bf16[128,128]{1,0:T(8,128)(2,1)} %w_out_hbm.1, f32[1,128]{1,0:T(1,128)} %bitcast.10, f32[1,128]{1,0:T(1,128)} %bitcast.11), custom_call_target="tpu_custom_call" | custom-call | flops 33554432 | bytes 1048576 | tf_op jit(solution)/shard_map/pallas_call | solution.py:224
  39.0 0.1 collective-permute-done.got_ref
  39.1 0.1 shard_map.121
  39.3 18.7 %all_to_all.11.t_ref = bf16[128,8,128]{2,1,0:T(8,128)(2,1)S(1)} all-to-all(bf16[128,8,128]{2,1,0:T(8,128)(2,1)S(1)} %bitcast.6), channel_id=1, replica_groups=mesh['y'=4,'zh'=2,'x'=4,'zl'=4,'core'=2] {'zl','zh','y','x'}, dimensions={0} | all-to-all | bytes 524288 | tf_op jit(solution)/shard_map/all_to_all | solution.py:243
  58.0 1.1 %shard_map.122 = bf16[16,64,128]{2,1,0:T(8,128)(2,1)} custom-call(bf16[128,8,128]{2,1,0:T(8,128)(2,1)S(1)} %all_to_all.11.t_ref, f32[16,64,128]{2,1,0:T(8,128)S(1)} %get-tuple-element.24.gate_ref, bf16[128,128]{1,0:T(8,128)(2,1)S(1)} %get-tuple-element.25.w_out, f32[2,128,128]{2,1,0:T(8,128)S(1)} %get-tuple-element.26.affine), custom_call_target="tpu_custom_call" | custom-call | tf_op jit(solution)/shard_map/pallas_call | solution.py:244
Async XLA Ops:
  34.6 4.5 %collective-permute-start = (bf16[512,256]{1,0:T(8,128)(2,1)S(1)}, bf16[512,256]{1,0:T(8,128)(2,1)S(1)}, u32[]{:S(2)}, u32[]{:S(2)}) collective-permute-start(bf16[512,256]{1,0:T(8,128)(2,1)S(1)} %get-tuple-element.23), channel_id=1, source_target_pairs={{0,1},{1,0},{2,3},{3,2},{4,5},{5,4},{6,7},{7,6},{8,9},{9,8},{10,11... | collective-permute-start | bytes 786440 | tf_op jit(solution)/shard_map/ppermute | solution.py:222

commit v6 on v5

--- a/solution.py
+++ b/solution.py
@@ -44,7 +44,10 @@
     for copy in copies:
         copy.wait()
     weights = jnp.concatenate([w_ref[n].T for n in range(4)], axis=0)
-    mask_k = mask_ref[pl.ds(lax.axis_index("zl"), 1), :].astype(F32)
+    mask_all = mask_ref[...].astype(F32)
+    mask_k = mask_all[:1]
+    for z in range(1, 4):
+        mask_k = jnp.where(lax.axis_index("zl") == z, mask_all[z : z + 1], mask_k)
     swapped = pltpu.roll(mask_k, 64, 1)
     low = low_lanes((1, 128))
     mask_k = jnp.where(low == (core == 0), mask_k, swapped)
@@ -69,7 +72,9 @@
             right = mask * jax.nn.sigmoid(p[384:]) * p[256:384]
             rows[pl.ds(s, 128, stride=8), :] = left
             rows[pl.ds(1024 + s, 128, stride=8), :] = right
-    out_ref[...] = jnp.concatenate([rows[:1024].reshape(128,8,128), rows[1024:].reshape(128,8,128)],axis=1).astype(BF16)
+    left = rows[:1024].reshape(128, 8, 128)
+    right = rows[1024:2048].reshape(128, 8, 128)
+    out_ref[...] = jnp.concatenate([left, right], axis=1).astype(BF16)
 
 
 def contract(s_ref, keep_ref, send_ref):
@@ -77,6 +82,7 @@
     edges = s_ref[...].astype(F32).reshape(4, 2, 4, 4, 16, 128)
     edges = jnp.stack([edges[:, 0], edges[:, 1]], axis=2).reshape(4, 32, 16, 128)
     low = low_lanes((256, 128))
+
     def halves(part):
         first, second = [], []
         for z in (0, 2):
@@ -129,7 +135,7 @@
 
 def finish(t_ref, gate_ref, w_out, affine, out_hbm, rows, out_ref, sems):
     t = t_ref[...].astype(F32)
-    rows[...] = t.reshape(1024, 128)
+    rows[:1024] = t.reshape(1024, 128)
     gain_col, bias_col = affine[0], affine[1]
     w = w_out[...]
     copies = []
@@ -201,7 +207,7 @@
             pltpu.VMEM((1, 128), F32),
             pltpu.VMEM((1, 128), F32),
             pltpu.VMEM((4, 128, 128), BF16),
-            pltpu.VMEM((2048, 128), F32),
+            pltpu.VMEM((2056, 128), F32),
             pltpu.SemaphoreType.DMA((9,)),
         ],
     )(
@@ -246,7 +252,7 @@
         shape(16, 64, 128),
         [VMEM] * 4,
         [
-            pltpu.VMEM((1024, 128), F32),
+            pltpu.VMEM((1032, 128), F32),
             pltpu.VMEM((16, 64, 128), BF16),
             pltpu.SemaphoreType.DMA((4,)),
         ],

time: 59.9 us -> 59.9 us (level)
  no operation moved by 1% of the time
where the time goes in v6:
time: 59.9 us; the launch traced here: 59.1 us
  blocking collectives  51 us (85%)
  Pallas kernels  4.65 us (8%)
  starting transfers between devices  3.32 us (6%)
    all_to_all x1, blocking collectives, shards(): edges = lax.all_to_all(edges, PEERS, 0, 0, tiled=True)  32.3 us
    all_to_all x1, blocking collectives, shards(): lax.all_to_all(triangle.reshape(128, 8, 128), PEERS, 0, 0, tiled=True)  18.7 us
    ppermute x1, starting transfers between devices, shards(): got = lax.ppermute(send, 'core', [(0, 1), (1, 0)])  3.32 us
    pallas_call x1, Pallas kernels, shards(): call(project, (shape(128, 16, 128), shape(16, 64, 128)), [HBM] * 9, [pltp...  1.9 us
  transfers between devices with their start and end apart: 1, of which 1 were waited for; matrix products, arithmetic and copies ran while one was open for 0% of the time, Pallas kernels for 2%

profile of v6, /device:TPU:1, one launch (start us, length us, event | category | flops | bytes accessed | tf_op | source)
XLA Modules:
  0.0 59.1 jit_solution(4963453137194249578)
XLA Ops:
  0.0 1.9 %shard_map.118 = (bf16[128,16,128]{2,1,0:T(8,128)(2,1)S(1)}, bf16[16,64,128]{2,1,0:T(8,128)(2,1)S(1)}) custom-call(bf16[16,64,128]{2,1,0:T(8,128)(2,1)} %x_hbm.1, s32[512]{0:T(512)} %mask_flat.1, s32[4,128]{1,0:T(4,128)} %bitcast.7, f32[1,128]{1,0:T(1,128)} %bitcast.8, f32[1,128]{1,0:T(1,128)} %bitcast.9, bf16[128,128]{1,0:T(8,128)(2,1)} %w_l.1, ...), custom_call_target="tpu_custom_call" | custom-call | tf_op jit(solution)/shard_map/pallas_call | solution.py:199
  1.9 32.3 %all_to_all.10.s_ref = bf16[128,16,128]{2,1,0:T(8,128)(2,1)S(1)} all-to-all(bf16[128,16,128]{2,1,0:T(8,128)(2,1)S(1)} %get-tuple-element.17), channel_id=1, replica_groups=mesh['y'=4,'zh'=2,'x'=4,'zl'=4,'core'=2] {'zl','zh','y','x'}, dimensions={0} | all-to-all | bytes 1048576 | tf_op jit(solution)/shard_map/all_to_all | solution.py:226
  34.2 0.4 shard_map.119
  34.6 3.3 %collective-permute-start = (bf16[512,256]{1,0:T(8,128)(2,1)S(1)}, bf16[512,256]{1,0:T(8,128)(2,1)S(1)}, u32[]{:S(2)}, u32[]{:S(2)}) collective-permute-start(bf16[512,256]{1,0:T(8,128)(2,1)S(1)} %get-tuple-element.23), channel_id=1, source_target_pairs={{0,1},{1,0},{2,3},{3,2},{4,5},{5,4},{6,7},{7,6},{8,9},{9,8},{10,11... | collective-permute-start | bytes 786440 | tf_op jit(solution)/shard_map/ppermute | solution.py:228
  38.0 1.0 %shard_map.120 = (f32[16,64,128]{2,1,0:T(8,128)S(1)}, bf16[128,128]{1,0:T(8,128)(2,1)S(1)}, f32[2,128,128]{2,1,0:T(8,128)S(1)}) custom-call(bf16[16,64,128]{2,1,0:T(8,128)(2,1)S(1)} %get-tuple-element.19.normed_ref, bf16[128,128]{1,0:T(8,128)(2,1)} %w_gate.1, bf16[128,128]{1,0:T(8,128)(2,1)} %w_out_hbm.1, f32[1,128]{1,0:T(1,128)} %bitcast.10, f32[1,128]{1,0:T(1,128)} %bitcast.11), custom_call_target="tpu_custom_call" | custom-call | flops 33554432 | bytes 1048576 | tf_op jit(solution)/shard_map/pallas_call | solution.py:230
  39.0 0.1 collective-permute-done.got_ref
  39.1 0.1 shard_map.121
  39.3 18.7 %all_to_all.11.t_ref = bf16[128,8,128]{2,1,0:T(8,128)(2,1)S(1)} all-to-all(bf16[128,8,128]{2,1,0:T(8,128)(2,1)S(1)} %bitcast.6), channel_id=1, replica_groups=mesh['y'=4,'zh'=2,'x'=4,'zl'=4,'core'=2] {'zl','zh','y','x'}, dimensions={0} | all-to-all | bytes 524288 | tf_op jit(solution)/shard_map/all_to_all | solution.py:249
  58.0 1.1 %shard_map.122 = bf16[16,64,128]{2,1,0:T(8,128)(2,1)} custom-call(bf16[128,8,128]{2,1,0:T(8,128)(2,1)S(1)} %all_to_all.11.t_ref, f32[16,64,128]{2,1,0:T(8,128)S(1)} %get-tuple-element.24.gate_ref, bf16[128,128]{1,0:T(8,128)(2,1)S(1)} %get-tuple-element.25.w_out, f32[2,128,128]{2,1,0:T(8,128)S(1)} %get-tuple-element.26.affine), custom_call_target="tpu_custom_call" | custom-call | tf_op jit(solution)/shard_map/pallas_call | solution.py:250
Async XLA Ops:
  34.6 4.5 %collective-permute-start = (bf16[512,256]{1,0:T(8,128)(2,1)S(1)}, bf16[512,256]{1,0:T(8,128)(2,1)S(1)}, u32[]{:S(2)}, u32[]{:S(2)}) collective-permute-start(bf16[512,256]{1,0:T(8,128)(2,1)S(1)} %get-tuple-element.23), channel_id=1, source_target_pairs={{0,1},{1,0},{2,3},{3,2},{4,5},{5,4},{6,7},{7,6},{8,9},{9,8},{10,11... | collective-permute-start | bytes 786440 | tf_op jit(solution)/shard_map/ppermute | solution.py:228

commit v7 on v6

--- a/solution.py
+++ b/solution.py
@@ -77,7 +77,7 @@
     out_ref[...] = jnp.concatenate([left, right], axis=1).astype(BF16)
 
 
-def contract(s_ref, keep_ref, send_ref):
+def contract(s_ref, send_ref, left_ref, mine_ref):
     core = lax.axis_index("core")
     edges = s_ref[...].astype(F32).reshape(4, 2, 4, 4, 16, 128)
     edges = jnp.stack([edges[:, 0], edges[:, 1]], axis=2).reshape(4, 32, 16, 128)
@@ -95,19 +95,22 @@
     right = halves(lambda z: edges[z, :, 8:].reshape(256, 128))
     both = jnp.concatenate([r.reshape(4, 2, 32, 256) for r in right], axis=2)
     first, second = both[:, 0].reshape(256, 256), both[:, 1].reshape(256, 256)
-    mine = jnp.where(core == 0, first, second)
+    left_ref[...] = left
+    mine_ref[...] = jnp.where(core == 0, first, second)
     other = jnp.where(core == 0, second, first)
     send_ref[...] = lax.dot_general(left, other, NT, preferred_element_type=F32).astype(BF16)
-    keep_ref[...] = lax.dot_general(left, mine, NT, preferred_element_type=F32)
 
 
 def prepare(
-    normed_ref, w_gate, w_out_hbm, gain_hbm, bias_hbm,
-    gate_ref, w_out_ref, affine_ref,
+    left_ref, mine_ref, normed_ref, w_gate, w_out_hbm, gain_hbm, bias_hbm,
+    keep_ref, gate_ref, w_out_ref, affine_ref,
     w_ref, gain, bias, sems,
 ):
     copies = fetch(
         (w_gate, w_out_hbm, gain_hbm, bias_hbm), (w_ref, w_out_ref, gain, bias), sems
+    )
+    keep_ref[...] = lax.dot_general(
+        left_ref[...], mine_ref[...], NT, preferred_element_type=F32
     )
     for copy in copies:
         copy.wait()
@@ -224,13 +227,19 @@
         )
     )
     edges = lax.all_to_all(edges, PEERS, 0, 0, tiled=True)
-    keep, send = call(contract, (shape(512, 256, dtype=F32), shape(512, 256)), [VMEM])(edges)
+    send, left, mine = call(
+        contract, (shape(512, 256), shape(512, 256), shape(256, 256)), [VMEM]
+    )(edges)
     got = lax.ppermute(send, "core", [(0, 1), (1, 0)])
-    normed, keep = lax.optimization_barrier((normed, keep))
-    gate, w_out, affine = call(
+    keep, gate, w_out, affine = call(
         prepare,
-        (shape(16, 64, 128, dtype=F32), shape(128, 128), shape(2, 128, 128, dtype=F32)),
-        [VMEM] + [HBM] * 4,
+        (
+            shape(512, 256, dtype=F32),
+            shape(16, 64, 128, dtype=F32),
+            shape(128, 128),
+            shape(2, 128, 128, dtype=F32),
+        ),
+        [VMEM] * 3 + [HBM] * 4,
         [
             pltpu.VMEM((128, 128), BF16),
             pltpu.VMEM((1, 128), F32),
@@ -238,13 +247,14 @@
             pltpu.SemaphoreType.DMA((4,)),
         ],
         cost=pl.CostEstimate(
-            flops=2 * 1024 * 128 * 128, bytes_accessed=1 << 20, transcendentals=1 << 18
+            flops=2 * 1024 * 128 * 128 + 2 * 512 * 256 * 256, bytes_accessed=1 << 20, transcendentals=1 << 18
         ),
     )(
+        left,
+        mine,
         normed,
         *in_hbm(w_gate, w_out, ln_out_gain.reshape(1, 128), ln_out_bias.reshape(1, 128)),
     )
-    gate, keep = lax.optimization_barrier((gate, keep))
     triangle = call(add_halves, shape(4, 2, 4, 4, 8, 128), [VMEM] * 2)(keep, got)
     triangle = lax.all_to_all(triangle.reshape(128, 8, 128), PEERS, 0, 0, tiled=True)
     return call(

time: 59.9 us -> 59.9 us (level)
  no operation moved by 1% of the time
where the time goes in v7:
time: 59.9 us; the launch traced here: 59 us
  blocking collectives  51 us (85%)
  Pallas kernels  4.64 us (8%)
  starting transfers between devices  3.32 us (6%)
    all_to_all x1, blocking collectives, shards(): edges = lax.all_to_all(edges, PEERS, 0, 0, tiled=True)  32.3 us
    all_to_all x1, blocking collectives, shards(): lax.all_to_all(triangle.reshape(128, 8, 128), PEERS, 0, 0, tiled=True)  18.7 us
    ppermute x1, starting transfers between devices, shards(): got = lax.ppermute(send, 'core', [(0, 1), (1, 0)])  3.32 us
    pallas_call x1, Pallas kernels, shards(): call(project, (shape(128, 16, 128), shape(16, 64, 128)), [HBM] * 9, [pltp...  1.9 us
  transfers between devices with their start and end apart: 1, of which 1 were waited for; matrix products, arithmetic and copies ran while one was open for 0% of the time, Pallas kernels for 2%

profile of v7, /device:TPU:1, one launch (start us, length us, event | category | flops | bytes accessed | tf_op | source)
XLA Modules:
  0.0 59.0 jit_solution(12350119033817919221)
XLA Ops:
  0.0 1.9 %shard_map.118 = (bf16[128,16,128]{2,1,0:T(8,128)(2,1)S(1)}, bf16[16,64,128]{2,1,0:T(8,128)(2,1)S(1)}) custom-call(bf16[16,64,128]{2,1,0:T(8,128)(2,1)} %x_hbm.1, s32[512]{0:T(512)} %mask_flat.1, s32[4,128]{1,0:T(4,128)} %bitcast.7, f32[1,128]{1,0:T(1,128)} %bitcast.8, f32[1,128]{1,0:T(1,128)} %bitcast.9, bf16[128,128]{1,0:T(8,128)(2,1)} %w_l.1, ...), custom_call_target="tpu_custom_call" | custom-call | tf_op jit(solution)/shard_map/pallas_call | solution.py:202
  1.9 32.3 %all_to_all.10.s_ref = bf16[128,16,128]{2,1,0:T(8,128)(2,1)S(1)} all-to-all(bf16[128,16,128]{2,1,0:T(8,128)(2,1)S(1)} %get-tuple-element.14), channel_id=1, replica_groups=mesh['y'=4,'zh'=2,'x'=4,'zl'=4,'core'=2] {'zl','zh','y','x'}, dimensions={0} | all-to-all | bytes 1048576 | tf_op jit(solution)/shard_map/all_to_all | solution.py:229
  34.2 0.4 shard_map.119
  34.6 3.3 %collective-permute-start = (bf16[512,256]{1,0:T(8,128)(2,1)S(1)}, bf16[512,256]{1,0:T(8,128)(2,1)S(1)}, u32[]{:S(2)}, u32[]{:S(2)}) collective-permute-start(bf16[512,256]{1,0:T(8,128)(2,1)S(1)} %get-tuple-element.19), channel_id=1, source_target_pairs={{0,1},{1,0},{2,3},{3,2},{4,5},{5,4},{6,7},{7,6},{8,9},{9,8},{10,11... | collective-permute-start | bytes 786440 | tf_op jit(solution)/shard_map/ppermute | solution.py:233
  37.9 1.1 %shard_map.120 = (f32[512,256]{1,0:T(8,128)S(1)}, f32[16,64,128]{2,1,0:T(8,128)S(1)}, bf16[128,128]{1,0:T(8,128)(2,1)S(1)}, f32[2,128,128]{2,1,0:T(8,128)S(1)}) custom-call(bf16[512,256]{1,0:T(8,128)(2,1)S(1)} %get-tuple-element.15.left_ref, bf16[256,256]{1,0:T(8,128)(2,1)S(1)} %get-tuple-element.16.mine_ref, ...), custom_call_target="tpu_custom_call" | custom-call | flops 100663296 | bytes 1048576 | tf_op jit(solution)/shard_map/pallas_call | solution.py:234
  39.0 0.1 collective-permute-done.got_ref
  39.0 0.1 shard_map.121
  39.2 18.7 %all_to_all.11.t_ref = bf16[128,8,128]{2,1,0:T(8,128)(2,1)S(1)} all-to-all(bf16[128,8,128]{2,1,0:T(8,128)(2,1)S(1)} %bitcast.6), channel_id=1, replica_groups=mesh['y'=4,'zh'=2,'x'=4,'zl'=4,'core'=2] {'zl','zh','y','x'}, dimensions={0} | all-to-all | bytes 524288 | tf_op jit(solution)/shard_map/all_to_all | solution.py:259
  57.9 1.1 %shard_map.122 = bf16[16,64,128]{2,1,0:T(8,128)(2,1)} custom-call(bf16[128,8,128]{2,1,0:T(8,128)(2,1)S(1)} %all_to_all.11.t_ref, f32[16,64,128]{2,1,0:T(8,128)S(1)} %get-tuple-element.20.gate_ref, bf16[128,128]{1,0:T(8,128)(2,1)S(1)} %get-tuple-element.21.w_out, f32[2,128,128]{2,1,0:T(8,128)S(1)} %get-tuple-element.22.affine), custom_call_target="tpu_custom_call" | custom-call | tf_op jit(solution)/shard_map/pallas_call | solution.py:260
Async XLA Ops:
  34.6 4.5 %collective-permute-start = (bf16[512,256]{1,0:T(8,128)(2,1)S(1)}, bf16[512,256]{1,0:T(8,128)(2,1)S(1)}, u32[]{:S(2)}, u32[]{:S(2)}) collective-permute-start(bf16[512,256]{1,0:T(8,128)(2,1)S(1)} %get-tuple-element.19), channel_id=1, source_target_pairs={{0,1},{1,0},{2,3},{3,2},{4,5},{5,4},{6,7},{7,6},{8,9},{9,8},{10,11... | collective-permute-start | bytes 786440 | tf_op jit(solution)/shard_map/ppermute | solution.py:233

commit v8 on v7

--- a/solution.py
+++ b/solution.py
@@ -77,41 +77,48 @@
     out_ref[...] = jnp.concatenate([left, right], axis=1).astype(BF16)
 
 
-def contract(s_ref, send_ref, left_ref, mine_ref):
-    core = lax.axis_index("core")
+def arrived(s_ref):
     edges = s_ref[...].astype(F32).reshape(4, 2, 4, 4, 16, 128)
-    edges = jnp.stack([edges[:, 0], edges[:, 1]], axis=2).reshape(4, 32, 16, 128)
-    low = low_lanes((256, 128))
-
-    def halves(part):
-        first, second = [], []
-        for z in (0, 2):
-            a, b = part(z), part(z + 1)
-            first.append(jnp.where(low, a, pltpu.roll(b, 64, 1)).astype(BF16))
-            second.append(jnp.where(low, pltpu.roll(a, 64, 1), b).astype(BF16))
-        return jnp.concatenate(first, axis=1), jnp.concatenate(second, axis=1)
-
-    left = jnp.concatenate(halves(lambda z: edges[z, :, :8].reshape(256, 128)), axis=0)
-    right = halves(lambda z: edges[z, :, 8:].reshape(256, 128))
-    both = jnp.concatenate([r.reshape(4, 2, 32, 256) for r in right], axis=2)
-    first, second = both[:, 0].reshape(256, 256), both[:, 1].reshape(256, 256)
+    return jnp.stack([edges[:, 0], edges[:, 1]], axis=2)
+
+
+def halves(part):
+    first, second = [], []
+    for z in (0, 2):
+        a, b = part(z), part(z + 1)
+        low = low_lanes(a.shape)
+        first.append(jnp.where(low, a, pltpu.roll(b, 64, 1)).astype(BF16))
+        second.append(jnp.where(low, pltpu.roll(a, 64, 1), b).astype(BF16))
+    return jnp.concatenate(first, axis=1), jnp.concatenate(second, axis=1)
+
+
+def right_rows(edges, first_half):
+    def part(z):
+        rows = jnp.where(first_half, edges[z, :, 0, :, 8:], edges[z, :, 1, :, 8:])
+        return rows.reshape(128, 128)
+
+    pair = [half.reshape(4, 32, 256) for half in halves(part)]
+    return jnp.concatenate(pair, axis=1).reshape(256, 256)
+
+
+def contract(s_ref, send_ref, left_ref):
+    edges = arrived(s_ref)
+    left = jnp.concatenate(halves(lambda z: edges[z, :, :, :, :8].reshape(256, 128)), axis=0)
     left_ref[...] = left
-    mine_ref[...] = jnp.where(core == 0, first, second)
-    other = jnp.where(core == 0, second, first)
+    other = right_rows(edges, lax.axis_index("core") == 1)
     send_ref[...] = lax.dot_general(left, other, NT, preferred_element_type=F32).astype(BF16)
 
 
 def prepare(
-    left_ref, mine_ref, normed_ref, w_gate, w_out_hbm, gain_hbm, bias_hbm,
+    left_ref, s_ref, normed_ref, w_gate, w_out_hbm, gain_hbm, bias_hbm,
     keep_ref, gate_ref, w_out_ref, affine_ref,
     w_ref, gain, bias, sems,
 ):
     copies = fetch(
         (w_gate, w_out_hbm, gain_hbm, bias_hbm), (w_ref, w_out_ref, gain, bias), sems
     )
-    keep_ref[...] = lax.dot_general(
-        left_ref[...], mine_ref[...], NT, preferred_element_type=F32
-    )
+    mine = right_rows(arrived(s_ref), lax.axis_index("core") == 0)
+    keep_ref[...] = lax.dot_general(left_ref[...], mine, NT, preferred_element_type=F32)
     for copy in copies:
         copy.wait()
     flat = normed_ref[...].reshape(1024, 128)
@@ -227,9 +234,7 @@
         )
     )
     edges = lax.all_to_all(edges, PEERS, 0, 0, tiled=True)
-    send, left, mine = call(
-        contract, (shape(512, 256), shape(512, 256), shape(256, 256)), [VMEM]
-    )(edges)
+    send, left = call(contract, (shape(512, 256), shape(512, 256)), [VMEM])(edges)
     got = lax.ppermute(send, "core", [(0, 1), (1, 0)])
     keep, gate, w_out, affine = call(
         prepare,
@@ -251,7 +256,7 @@
         ),
     )(
         left,
-        mine,
+        edges,
         normed,
         *in_hbm(w_gate, w_out, ln_out_gain.reshape(1, 128), ln_out_bias.reshape(1, 128)),
     )

time: 59.9 us -> 59.9 us (level)
  no operation moved by 1% of the time
where the time goes in v8:
time: 59.9 us; the launch traced here: 59 us
  blocking collectives  51 us (85%)
  Pallas kernels  4.63 us (8%)
  starting transfers between devices  3.32 us (6%)
    all_to_all x1, blocking collectives, shards(): edges = lax.all_to_all(edges, PEERS, 0, 0, tiled=True)  32.3 us
    all_to_all x1, blocking collectives, shards(): lax.all_to_all(triangle.reshape(128, 8, 128), PEERS, 0, 0, tiled=True)  18.7 us
    ppermute x1, starting transfers between devices, shards(): got = lax.ppermute(send, 'core', [(0, 1), (1, 0)])  3.32 us
    pallas_call x1, Pallas kernels, shards(): call(project, (shape(128, 16, 128), shape(16, 64, 128)), [HBM] * 9, [pltp...  1.9 us
  transfers between devices with their start and end apart: 1, of which 1 were waited for; matrix products, arithmetic and copies ran while one was open for 0% of the time, Pallas kernels for 2%

profile of v8, /device:TPU:1, one launch (start us, length us, event | category | flops | bytes accessed | tf_op | source)
XLA Modules:
  0.0 59.0 jit_solution(6468067595628303636)
XLA Ops:
  0.0 1.9 %shard_map.118 = (bf16[128,16,128]{2,1,0:T(8,128)(2,1)S(1)}, bf16[16,64,128]{2,1,0:T(8,128)(2,1)S(1)}) custom-call(bf16[16,64,128]{2,1,0:T(8,128)(2,1)} %x_hbm.1, s32[512]{0:T(512)} %mask_flat.1, s32[4,128]{1,0:T(4,128)} %bitcast.7, f32[1,128]{1,0:T(1,128)} %bitcast.10, f32[1,128]{1,0:T(1,128)} %bitcast.11, bf16[128,128]{1,0:T(8,128)(2,1)} %w_l.1, ...), custom_call_target="tpu_custom_call" | custom-call | tf_op jit(solution)/shard_map/pallas_call | solution.py:209
  1.9 32.3 %all_to_all.10.s_ref = bf16[128,16,128]{2,1,0:T(8,128)(2,1)S(1)} all-to-all(bf16[128,16,128]{2,1,0:T(8,128)(2,1)S(1)} %get-tuple-element.13), channel_id=1, replica_groups=mesh['y'=4,'zh'=2,'x'=4,'zl'=4,'core'=2] {'zl','zh','y','x'}, dimensions={0} | all-to-all | bytes 1048576 | tf_op jit(solution)/shard_map/all_to_all | solution.py:236
  34.2 0.4 shard_map.119
  34.6 3.3 %collective-permute-start = (bf16[512,256]{1,0:T(8,128)(2,1)S(1)}, bf16[512,256]{1,0:T(8,128)(2,1)S(1)}, u32[]{:S(2)}, u32[]{:S(2)}) collective-permute-start(bf16[512,256]{1,0:T(8,128)(2,1)S(1)} %get-tuple-element.17), channel_id=1, source_target_pairs={{0,1},{1,0},{2,3},{3,2},{4,5},{5,4},{6,7},{7,6},{8,9},{9,8},{10,11... | collective-permute-start | bytes 786440 | tf_op jit(solution)/shard_map/ppermute | solution.py:238
  37.9 1.1 %shard_map.120 = (f32[512,256]{1,0:T(8,128)S(1)}, f32[16,64,128]{2,1,0:T(8,128)S(1)}, bf16[128,128]{1,0:T(8,128)(2,1)S(1)}, f32[2,128,128]{2,1,0:T(8,128)S(1)}) custom-call(bf16[512,256]{1,0:T(8,128)(2,1)S(1)} %get-tuple-element.14.left_ref, bf16[128,16,128]{2,1,0:T(8,128)(2,1)S(1)} %all_to_all.10.s_ref, ...), custom_call_target="tpu_custom_call" | custom-call | flops 100663296 | bytes 1048576 | tf_op jit(solution)/shard_map/pallas_call | solution.py:239
  39.0 0.1 collective-permute-done.got_ref
  39.0 0.1 shard_map.121
  39.2 18.7 %all_to_all.11.t_ref = bf16[128,8,128]{2,1,0:T(8,128)(2,1)S(1)} all-to-all(bf16[128,8,128]{2,1,0:T(8,128)(2,1)S(1)} %bitcast.6), channel_id=1, replica_groups=mesh['y'=4,'zh'=2,'x'=4,'zl'=4,'core'=2] {'zl','zh','y','x'}, dimensions={0} | all-to-all | bytes 524288 | tf_op jit(solution)/shard_map/all_to_all | solution.py:264
  57.9 1.1 %shard_map.122 = bf16[16,64,128]{2,1,0:T(8,128)(2,1)} custom-call(bf16[128,8,128]{2,1,0:T(8,128)(2,1)S(1)} %all_to_all.11.t_ref, f32[16,64,128]{2,1,0:T(8,128)S(1)} %get-tuple-element.18.gate_ref, bf16[128,128]{1,0:T(8,128)(2,1)S(1)} %get-tuple-element.19.w_out, f32[2,128,128]{2,1,0:T(8,128)S(1)} %get-tuple-element.20.affine), custom_call_target="tpu_custom_call" | custom-call | tf_op jit(solution)/shard_map/pallas_call | solution.py:265
Async XLA Ops:
  34.6 4.5 %collective-permute-start = (bf16[512,256]{1,0:T(8,128)(2,1)S(1)}, bf16[512,256]{1,0:T(8,128)(2,1)S(1)}, u32[]{:S(2)}, u32[]{:S(2)}) collective-permute-start(bf16[512,256]{1,0:T(8,128)(2,1)S(1)} %get-tuple-element.17), channel_id=1, source_target_pairs={{0,1},{1,0},{2,3},{3,2},{4,5},{5,4},{6,7},{7,6},{8,9},{9,8},{10,11... | collective-permute-start | bytes 786440 | tf_op jit(solution)/shard_map/ppermute | solution.py:238
